TPU v7x, 128 devices: a whole 4x4x4 slice. The times are simulated.
128 devices in a mesh: dp: 32 (over z_lo, x, y), tensor: 4 (over z_hi, core).
Axes of the slice: x: 4, y: 4, z: 4 (z_hi: 2, z_lo: 2; z = z_hi * 2 + z_lo), core: 2. Of those that a mesh axis runs over, the one named last changes fastest.
Arguments:
- hidden_in: bfloat16 [16384, 2048], P('dp'), may hold values from -6 to 6
- segment_ids: int32 [16384], P('dp'), may hold values from 0 to 3, as said below
- positions: int32 [16384], P('dp'), may hold values from 0 to 508, as said below
- ln1_gain: float32 [2048], replicated, may hold values from 0.1 to 1.9
- ln1_bias: float32 [2048], replicated, may hold values from -3 to 3
- qkv_weight: bfloat16 [2048, 6144], P(None, 'tensor'), may hold values from -0.125 to 0.125
- qkv_bias: float32 [8, 768], P('tensor'), may hold values from -3 to 3
- dense_weight: bfloat16 [2048, 2048], P('tensor'), may hold values from -0.5 to 0.5
- dense_bias: float32 [2048], replicated, may hold values from -3 to 3
- ln2_gain: float32 [2048], replicated, may hold values from 0.1 to 1.9
- ln2_bias: float32 [2048], replicated, may hold values from -3 to 3
- fc1_weight: bfloat16 [2048, 8192], P(None, 'tensor'), may hold values from -0.125 to 0.125
- fc1_bias: float32 [64, 128], P('tensor'), may hold values from -3 to 3
- fc2_weight: bfloat16 [8192, 2048], P('tensor'), may hold values from -0.0625 to 0.0625
- fc2_bias: float32 [2048], replicated, may hold values from -3 to 3
- cotangent: bfloat16 [16384, 2048], P('dp'), may hold values from -6 to 6
Outputs:
- output: float32 [16384, 2048], P('dp')
- input_grad: float32 [16384, 2048], P('dp')
- ln1_gain_grad: float32 [2048], P('dp')
- ln1_bias_grad: float32 [2048], P('dp')
- qkv_weight_grad: float32 [2048, 6144], P('dp', 'tensor')
- qkv_bias_grad: float32 [8, 768], P('tensor', 'dp')
- dense_weight_grad: float32 [2048, 2048], P('tensor', 'dp')
- dense_bias_grad: float32 [2048], P('dp')
- ln2_gain_grad: float32 [2048], P('dp')
- ln2_bias_grad: float32 [2048], P('dp')
- fc1_weight_grad: float32 [2048, 8192], P('dp', 'tensor')
- fc1_bias_grad: float32 [64, 128], P('tensor', 'dp')
- fc2_weight_grad: float32 [8192, 2048], P('tensor', 'dp')
- fc2_bias_grad: float32 [2048], P('dp')
Inputs may be any that keep to these rules, and one draw needn't show every extreme that they name: `segment_ids`: within each sequence of 512 tokens the segment numbers start at 0, never fall, and take each of the 4 values. `positions`: A token's index in its sequence minus the index of its document's first token.
All inputs are finite; a program needn't handle non-finite values.
Results may differ from a plain program's by a relative error of at most 0.011.
Values sent between devices are 32-bit elements; how exact they have to be, the bound alone decides.
No kernel may reach another device: no remote copies, remote signals or barrier semaphores. Data moves between devices by JAX's collectives and lax.ppermute only.
A program may use at most 256 MiB of HBM per device.

v0:
```python
from functools import partial
import math

import jax
import jax.numpy as jnp
from jax import lax
from jax.sharding import PartitionSpec as P

HD = 256
ROT = 64


EPSILON = 1e-05
NEGATIVE = -1000000000.0


def angle_tables(positions):
    halves = jnp.arange(ROT // 2, dtype=jnp.float32)
    inverse = 10000.0 ** (-2.0 * halves / ROT)
    angles = positions.astype(jnp.float32)[..., None] * inverse
    angles = jnp.concatenate([angles, angles], axis=-1)
    return (jnp.cos(angles), jnp.sin(angles))


def rotate(vectors, cosine, sine):
    turned = vectors[..., :ROT]
    first = turned[..., : ROT // 2]
    second = turned[..., ROT // 2 :]
    swapped = jnp.concatenate([-second, first], axis=-1)
    return jnp.concatenate([turned * cosine + swapped * sine, vectors[..., ROT:]], axis=-1)


def plain_dot(left, right):
    return jnp.dot(left, right, preferred_element_type=jnp.float32)


def contract_rows(left, right):
    return lax.dot_general(
        left, right, (((0,), (0,)), ((), ())), preferred_element_type=jnp.float32
    )


def contract_cols(left, right):
    return lax.dot_general(
        left, right, (((1,), (1,)), ((), ())), preferred_element_type=jnp.float32
    )


def masked_scores(queries, keys_rot, segments):
    scores = jnp.einsum("qhd,khd->hqk", queries, keys_rot, preferred_element_type=jnp.float32) * (
        1.0 / math.sqrt(HD)
    )
    order = jnp.arange(segments.shape[0])
    allowed = (segments[:, None] == segments[None, :]) & (order[None, :] <= order[:, None])
    return jnp.where(allowed[None], scores, NEGATIVE)


def body(
    hidden_in,
    segment_ids,
    positions,
    ln1_gain,
    ln1_bias,
    qkv_weight,
    qkv_bias,
    dense_weight,
    dense_bias,
    ln2_gain,
    ln2_bias,
    fc1_weight,
    fc1_bias,
    fc2_weight,
    fc2_bias,
    cotangent,
):
    hidden = hidden_in.astype(jnp.float32)
    tokens = hidden.shape[0]
    heads = qkv_weight.shape[1] // (3 * HD)
    average = jnp.mean(hidden, axis=-1, keepdims=True)
    centred = hidden - average
    inv_std = lax.rsqrt(jnp.mean(centred * centred, axis=-1, keepdims=True) + EPSILON)
    normed = centred * inv_std
    first_in = (normed * ln1_gain + ln1_bias).astype(jnp.bfloat16)
    second_in = (normed * ln2_gain + ln2_bias).astype(jnp.bfloat16)
    packed = (plain_dot(first_in, qkv_weight) + qkv_bias.reshape(-1)).reshape(tokens, heads, 3, HD)
    cosine, sine = angle_tables(positions)
    cosine = cosine[:, None, :]
    sine = sine[:, None, :]
    queries = rotate(packed[:, :, 0], cosine, sine).astype(jnp.bfloat16)
    keys_rot = rotate(packed[:, :, 1], cosine, sine).astype(jnp.bfloat16)
    values_in = packed[:, :, 2].astype(jnp.bfloat16)
    scores = masked_scores(queries, keys_rot, segment_ids)
    top = jnp.max(scores, axis=-1, keepdims=True)
    weights = jnp.exp(scores - top)
    totals = jnp.sum(weights, axis=-1, keepdims=True)
    log_total = top + jnp.log(totals)
    probs_low = (weights / totals).astype(jnp.bfloat16)
    mixed = jnp.einsum("hqk,khd->qhd", probs_low, values_in, preferred_element_type=jnp.float32)
    mixed_low = mixed.reshape(tokens, heads * HD).astype(jnp.bfloat16)
    attn_part = plain_dot(mixed_low, dense_weight)
    upward = plain_dot(second_in, fc1_weight) + fc1_bias.reshape(-1)
    act_low = jax.nn.gelu(upward, approximate=False).astype(jnp.bfloat16)
    mlp_part = plain_dot(act_low, fc2_weight)
    branches = lax.psum(attn_part, "tensor") + lax.psum(mlp_part, "tensor")
    output = hidden + branches + dense_bias + fc2_bias
    grad_out = cotangent.astype(jnp.float32)
    bias_sum = jnp.sum(grad_out, axis=0)
    dense_grad = contract_rows(mixed_low, cotangent)
    down_grad = contract_rows(act_low, cotangent)
    grad_mixed = (
        contract_cols(cotangent, dense_weight).astype(jnp.bfloat16).reshape(tokens, heads, HD)
    )
    grad_act = contract_cols(cotangent, fc2_weight)
    _, gelu_back = jax.vjp(partial(jax.nn.gelu, approximate=False), upward)
    grad_up = gelu_back(grad_act)[0].astype(jnp.bfloat16)
    up_bias_grad = jnp.sum(grad_up.astype(jnp.float32), axis=0).reshape(fc1_bias.shape)
    up_grad = contract_rows(second_in, grad_up)
    second_part = contract_cols(grad_up, fc1_weight)
    again = masked_scores(queries, keys_rot, segment_ids)
    probs = jnp.exp(again - log_total)
    grad_probs = jnp.einsum(
        "qhd,khd->hqk", grad_mixed, values_in, preferred_element_type=jnp.float32
    )
    along = jnp.sum(probs * grad_probs, axis=-1, keepdims=True)
    grad_scores = (probs * (grad_probs - along)).astype(jnp.bfloat16)
    score_scale = 1.0 / math.sqrt(HD)
    grad_query = (
        jnp.einsum("hqk,khd->qhd", grad_scores, keys_rot, preferred_element_type=jnp.float32)
        * score_scale
    )
    grad_key = (
        jnp.einsum("hqk,qhd->khd", grad_scores, queries, preferred_element_type=jnp.float32)
        * score_scale
    )
    grad_value = jnp.einsum(
        "hqk,qhd->khd", probs_low, grad_mixed, preferred_element_type=jnp.float32
    )
    grad_packed = jnp.stack(
        [rotate(grad_query, cosine, -sine), rotate(grad_key, cosine, -sine), grad_value], axis=2
    )
    grad_packed = grad_packed.reshape(tokens, heads * 3 * HD).astype(jnp.bfloat16)
    qkv_bias_sum = jnp.sum(grad_packed.astype(jnp.float32), axis=0).reshape(qkv_bias.shape)
    qkv_grad = contract_rows(first_in, grad_packed)
    first_part = contract_cols(grad_packed, qkv_weight)
    first_total, second_total = lax.psum((first_part, second_part), "tensor")
    gain_one_grad = jnp.sum(first_total * normed, axis=0)
    shift_one_grad = jnp.sum(first_total, axis=0)
    gain_two_grad = jnp.sum(second_total * normed, axis=0)
    shift_two_grad = jnp.sum(second_total, axis=0)
    combined = first_total * ln1_gain + second_total * ln2_gain
    input_grad = grad_out + inv_std * (
        combined
        - jnp.mean(combined, axis=-1, keepdims=True)
        - normed * jnp.mean(combined * normed, axis=-1, keepdims=True)
    )
    (
        gain_one_sum,
        shift_one_sum,
        qkv_sum,
        qkv_bias_total,
        dense_sum,
        bias_total,
        gain_two_sum,
        shift_two_sum,
        up_sum,
        up_bias_sum,
        down_sum,
    ) = (
        lax.psum_scatter(gain_one_grad, "dp", scatter_dimension=0, tiled=True),
        lax.psum_scatter(shift_one_grad, "dp", scatter_dimension=0, tiled=True),
        lax.psum_scatter(qkv_grad, "dp", scatter_dimension=0, tiled=True),
        lax.psum_scatter(qkv_bias_sum, "dp", scatter_dimension=1, tiled=True),
        lax.psum_scatter(dense_grad, "dp", scatter_dimension=1, tiled=True),
        lax.psum_scatter(bias_sum, "dp", scatter_dimension=0, tiled=True),
        lax.psum_scatter(gain_two_grad, "dp", scatter_dimension=0, tiled=True),
        lax.psum_scatter(shift_two_grad, "dp", scatter_dimension=0, tiled=True),
        lax.psum_scatter(up_grad, "dp", scatter_dimension=0, tiled=True),
        lax.psum_scatter(up_bias_grad, "dp", scatter_dimension=1, tiled=True),
        lax.psum_scatter(down_grad, "dp", scatter_dimension=1, tiled=True),
    )
    return (
        output,
        input_grad,
        gain_one_sum,
        shift_one_sum,
        qkv_sum,
        qkv_bias_total,
        dense_sum,
        bias_total,
        gain_two_sum,
        shift_two_sum,
        up_sum,
        up_bias_sum,
        down_sum,
        bias_total,
    )


def solution(mesh):
    return jax.shard_map(
        body,
        mesh=mesh,
        in_specs=(
            P("dp", None),
            P("dp"),
            P("dp"),
            P(),
            P(),
            P(None, "tensor"),
            P("tensor", None),
            P("tensor", None),
            P(),
            P(),
            P(),
            P(None, "tensor"),
            P("tensor", None),
            P("tensor", None),
            P(),
            P("dp", None),
        ),
        out_specs=(
            P("dp", None),
            P("dp", None),
            P("dp"),
            P("dp"),
            P("dp", "tensor"),
            P("tensor", "dp"),
            P("tensor", "dp"),
            P("dp"),
            P("dp"),
            P("dp"),
            P("dp", "tensor"),
            P("tensor", "dp"),
            P("tensor", "dp"),
            P("dp"),
        ),
        check_vma=False,
    )
```

profile of v0, /device:TPU:0, one launch (start us, length us, event | category | flops | bytes accessed | tf_op | source)
XLA Modules:
  0.0 887.3 jit_solution(8296648723511658109)
XLA Ops:
  8.1 2.1 convert_reduce_fusion
  10.2 2.3 fusion.17
  12.5 8.6 convolution_add_fusion.1
  21.1 3.8 copy.61
  24.9 3.0 fusion.57
  28.0 1.6 copy.92
  29.5 1.0 slice.129
  30.6 2.5 copy.93
  33.1 1.5 slice.128
  34.6 1.6 slice_negate_fusion.2
  36.6 1.1 fusion.45
  38.2 0.8 fusion.58
  39.8 1.4 convolution_convert_fusion
  41.9 0.8 multiply_convert_fusion.1
  46.8 1.5 convert_reduce_fusion.3
  48.2 3.1 copy.76
  51.4 8.8 fusion.60
  60.3 7.2 fusion.48
  67.5 14.6 %convert_reduce_fusion.2 = (f32[2048]{0:T(1024)S(1)}, bf16[512,2048]{1,0:T(8,128)(2,1)S(1)}, f32[512,2048]{1,0:T(8,128)S(1)}) fusion(f32[512,2048]{1,0:T(8,128)S(1)} %fusion.48, f32[2048]{0:T(1024)S(1)} %bitcast.77, bf16[512,2048]{1,0:T(8,128)(2,1)S(1)} %copy-done.6, bf16[2048,2048]{1,0:T(8,128)(2,1)S(1)} %bitcast.80), kind=kOutput, calls=%fused_computation.27 | convolution fusion | flops 4373608448 | bytes 20987904 | tf_op jit(solution)/shard_map/dot_general | solution.py:44
  82.2 1.0 multiply_convert_fusion
  83.2 4.5 fusion.59
  87.8 9.6 %fusion.61 = f32[512,2048]{1,0:T(8,128)} fusion(bf16[512,2048]{1,0:T(8,128)(2,1)S(1)} %get-tuple-element.59, bf16[2048,2048]{1,0:T(8,128)(2,1)} %param.27), kind=kOutput, calls=%fused_computation.117 | convolution fusion | flops 4294967296 | bytes 14680064 | tf_op jit(solution)/shard_map/dot_general | solution.py:44
  97.4 3.4 convolution_add_fusion
  100.9 4.8 fusion.62
  105.8 10.9 %fusion.50 = f32[2048,1536]{1,0:T(8,128)} fusion(bf16[512,1536]{0,1:T(8,128)(2,1)} %bitcast.74, bf16[512,2048]{1,0:T(8,128)(2,1)} %param.16, f32[2048]{0:T(1024)S(1)} %copy-done.18, f32[2048]{0:T(1024)S(1)} %copy-done.11, f32[512]{0:T(512)S(1)} %add_rsqrt_fusion, f32[512]{0:T(512)S(1)} %broadcast_multiply_fusion.3), kind=kOutput, calls=%fused_computation.109 | convolution fusion | flops 3227516928 | bytes 16273408 | tf_op jit(solution)/shard_map/dot_general | solution.py:38
  116.7 12.8 %fusion.46 = f32[2048,2048]{1,0:T(8,128)} fusion(bf16[512,2048]{1,0:T(8,128)(2,1)} %copy-done.22, bf16[512,2048]{1,0:T(8,128)(2,1)} %param.16, f32[2048]{0:T(1024)S(1)} %copy-done.19, f32[2048]{0:T(1024)S(1)} %copy-done.10, f32[512]{0:T(512)S(1)} %add_rsqrt_fusion, f32[512]{0:T(512)S(1)} %broadcast_multiply_fusion.3), kind=kOutput, calls=%fused_computation.107 | convolution fusion | flops 4301258752 | bytes 20992000 | tf_op jit(solution)/shard_map/dot_general | solution.py:38
  129.8 12.5 %fusion.63 = f32[2048,2048]{0,1:T(8,128)} fusion(bf16[512,2048]{1,0:T(8,128)(2,1)} %copy-done.9, bf16[512,2048]{1,0:T(8,128)(2,1)} %param.31), kind=kOutput, calls=%fused_computation.119 | convolution fusion | flops 4294967296 | bytes 20971520 | tf_op jit(solution)/shard_map/dot_general | solution.py:38
  145.5 532.5 %all-reduce.11.cloned.1.call-done = (f32[512,2048]{1,0:T(8,128)}, f32[512,2048]{1,0:T(8,128)}, f32[512,2048]{1,0:T(8,128)}) async-done(((f32[512,2048]{1,0:T(8,128)}, f32[512,2048]{1,0:T(8,128)}, f32[512,2048]{1,0:T(8,128)}), (f32[512,2048]{1,0:T(8,128)}, f32[512,2048]{1,0:T(8,128)}, f32[512,2048]{1,0:T(8,128)})) %all-reduce.11.cloned.1.call-update) | async-done | bytes 12582928 | tf_op jit(solution)/shard_map/psum | solution.py:104
  678.0 8.3 fusion.53
  686.3 3.4 convert_reduce_fusion.1
  689.7 158.4 %all-reduce.7 = (f32[2048]{0:T(1024)S(1)}, f32[2048]{0:T(1024)S(1)}, f32[2,768]{1,0:T(2,128)S(1)}, f32[2048]{0:T(1024)S(1)}, f32[2048]{0:T(1024)S(1)}, /*index=5*/f32[2048]{0:T(1024)S(1)}, f32[16,128]{1,0:T(8,128)S(1)}) all-reduce(f32[2048]{0:T(1024)S(1)} %get-tuple-element.67, ...), channel_id=2, replica_groups=mesh['dp'=32,'tensor'=4] {'dp'}, use_global_device_ids=true, to_apply=%region_12.13.clone | all-reduce | flops 13824 | bytes 110592
  851.9 27.0 %reduce-scatter.13.cloned.1.call-done = f32[2048,64]{0,1:T(8,128)} async-done(((f32[2048,2048]{0,1:T(8,128)}), f32[2048,64]{0,1:T(8,128)}) %reduce-scatter.13.cloned.1.call-update) | async-done | bytes 524304 | tf_op jit(solution)/shard_map/reduce_scatter | solution.py:179
  (98 shorter events, 12.4 us)
Async XLA Ops:
  8.0 31.3 %copy-start = (bf16[512,2048]{1,0:T(8,128)(2,1)S(1)}, bf16[512,2048]{1,0:T(8,128)(2,1)}, u32[]{:S(2)}) copy-start(bf16[512,2048]{1,0:T(8,128)(2,1)} %param.23) | copy-start | bytes 6291460
  8.0 4.5 copy-start.16
  8.0 4.5 copy-start.11
  8.0 4.5 copy-start.18
  8.1 669.9 %all-reduce.11.cloned.1.call-start = ((), (), s32[]{:S(2)}) async-start(), calls=%async_computation.8 | async-start | bytes 25165824 | tf_op jit(solution)/shard_map/psum | solution.py:104
  29.5 6.7 copy-start.17
  29.5 6.7 copy-start.14
  33.1 4.7 copy-start.4
  34.6 3.6 copy-start.8
  38.2 1.6 copy-start.5
  39.3 2.0 copy-start.3
  51.3 8.9 %copy-start.1 = (bf16[512,2048]{1,0:T(8,128)(2,1)S(1)}, bf16[512,2048]{1,0:T(8,128)(2,1)}, u32[]{:S(2)}) copy-start(bf16[512,2048]{1,0:T(8,128)(2,1)} %param.16) | copy-start | bytes 6291460
  51.4 8.9 copy-start.10
  51.4 8.9 copy-start.19
  51.4 16.1 %slice-start = ((s8[8388608]{0:T(1024)(128)(4,1)}), s8[4194304]{0:T(1024)(128)(4,1)S(1)}, s32[]{:S(2)}) async-start(s8[8388608]{0:T(1024)(128)(4,1)} %bitcast.79), calls=%async_computation.9 | async-start | bytes 8388608
  60.2 7.3 copy-start.6
  60.2 7.3 copy-start.15
  60.2 7.3 slice-start.1
  82.2 5.6 copy-start.22
  83.2 4.5 copy-start.9
  100.8 751.0 %reduce-scatter.9.cloned.1.call-start = ((), (), s32[]{:S(2)}) async-start(), calls=%async_computation.5 | async-start | bytes 4325376 | tf_op jit(solution)/shard_map/reduce_scatter | solution.py:173
  105.7 746.1 %reduce-scatter.7.cloned.1.call-start = ((), (), s32[]{:S(2)}) async-start(), calls=%async_computation.4 | async-start | bytes 12976128 | tf_op jit(solution)/shard_map/reduce_scatter | solution.py:171
  116.7 735.2 %reduce-scatter.11.cloned.1.call-start = ((), (), s32[]{:S(2)}) async-start(), calls=%async_computation.6 | async-start | bytes 17301504 | tf_op jit(solution)/shard_map/reduce_scatter | solution.py:177
  129.5 749.4 %reduce-scatter.13.cloned.1.call-start = ((), (), s32[]{:S(2)}) async-start(), calls=%async_computation.7 | async-start | bytes 17301504 | tf_op jit(solution)/shard_map/reduce_scatter | solution.py:179
  142.3 0.7 copy-start.20
  142.3 535.7 %copy-start.12 = (f32[2048]{0:T(1024)S(1)}, f32[2048]{0:T(1024)}, u32[]{:S(2)}) copy-start(f32[2048]{0:T(1024)} %param.30) | copy-start | bytes 24580
  142.3 535.7 %copy-start.13 = (f32[2048]{0:T(1024)S(1)}, f32[2048]{0:T(1024)}, u32[]{:S(2)}) copy-start(f32[2048]{0:T(1024)} %param.24) | copy-start | bytes 24580
  678.0 8.3 copy-start.2
  678.0 8.3 copy-start.7
  848.7 30.7 %copy-start.21 = (f32[64]{0:T(128)}, f32[64]{0:T(128)S(1)}, u32[]{:S(2)}) copy-start(f32[64]{0:T(128)S(1)} %dynamic-slice.7) | copy-start | bytes 772
Sparse Core Ops, SparseCore 0:
  100.9 576.9 all-reduce.10
Sparse Core Ops, SparseCore 1:
  105.8 172.2 reduce-scatter.8
  280.9 185.9 reduce-scatter.6
  469.6 202.5 reduce-scatter.10
  675.2 203.7 reduce-scatter.12
where the time goes:
time: 891 us; the launch traced here: 887 us
  waiting for transfers between devices  560 us (63%)
  blocking collectives  158 us (18%)
  matrix products  103 us (12%)
  other arithmetic  24.5 us (3%)
  local copies, waits for them, and re-layouts  23.2 us (3%)
  between operations  18.4 us (2%)
    psum x1, waiting for transfers between devices, body(): branches = lax.psum(attn_part, 'tensor') + lax.psum(mlp_part, 'tensor')  532 us
    unnamed x1, blocking collectives  158 us
    dot_general x4, matrix products, contract_rows(): lax.dot_general(left, right, (((0,), (0,)), ((), ())), preferred_element_...  41 us
    dot_general x4, matrix products, contract_cols(): lax.dot_general(left, right, (((1,), (1,)), ((), ())), preferred_element_...  34.5 us
    reduce_scatter x1, waiting for transfers between devices, body(): lax.psum_scatter(down_grad, 'dp', scatter_dimension=1, tiled=True)  27 us
    dot_general x4, matrix products, plain_dot(): return jnp.dot(left, right, preferred_element_type=jnp.float32)  23.7 us
  transfers between devices with their start and end apart: 5, of which 2 were waited for; matrix products, arithmetic and copies ran while one was open for 6% of the time, Pallas kernels for 0%

commit v1 on v0

v1 whole, which is shorter than its diff:
```python
from functools import partial
import math

import jax
import jax.numpy as jnp
from jax import lax
from jax.experimental import pallas as pl
from jax.experimental.pallas import tpu as pltpu
from jax.sharding import Mesh, PartitionSpec as P

HD = 256
ROT = 64
TOK = 512
D = 2048
EPSILON = 1e-05
NEGATIVE = -1000000000.0
SIZES = {"zl": 2, "x": 4, "y": 4, "zh": 2, "c": 2}
DP = ("zl", "x", "y")
TENSOR = ("zh", "c")
F32 = jnp.float32
BF16 = jnp.bfloat16


def send(value, axis, step=1):
    n = SIZES[axis]
    return lax.ppermute(value, axis, [(i, (i + step) % n) for i in range(n)])


def angle_tables(positions):
    halves = jnp.arange(ROT // 2, dtype=F32)
    inverse = 10000.0 ** (-2.0 * halves / ROT)
    angles = positions.astype(F32)[..., None] * inverse
    angles = jnp.concatenate([angles, angles], axis=-1)
    return (jnp.cos(angles), jnp.sin(angles))


def rotate(vectors, cosine, sine):
    turned = vectors[..., :ROT]
    first = turned[..., : ROT // 2]
    second = turned[..., ROT // 2 :]
    swapped = jnp.concatenate([-second, first], axis=-1)
    return jnp.concatenate([turned * cosine + swapped * sine, vectors[..., ROT:]], axis=-1)


def plain_dot(left, right):
    return jnp.dot(left, right, preferred_element_type=F32)


def contract_cols(left, right):
    return lax.dot_general(left, right, (((1,), (1,)), ((), ())), preferred_element_type=F32)


def masked_scores(queries, keys_rot, segments):
    scores = jnp.einsum("qhd,khd->hqk", queries, keys_rot, preferred_element_type=F32) * (
        1.0 / math.sqrt(HD)
    )
    order = jnp.arange(segments.shape[0])
    allowed = (segments[:, None] == segments[None, :]) & (order[None, :] <= order[:, None])
    return jnp.where(allowed[None], scores, NEGATIVE)


def turn_kernel(place, source, target, turned):
    turned[...] = source[...].astype(F32).T.astype(BF16)
    for ky in range(4):
        start = pl.multiple_of(lax.rem(place[2] + ky, 4) * 64, 64)
        target[0, 0, ky] = turned[pl.ds(start, 64), :]


def turned_rows(values, place):
    return pl.pallas_call(
        turn_kernel,
        grid_spec=pltpu.PrefetchScalarGridSpec(
            num_scalar_prefetch=1,
            grid=(2, 4),
            in_specs=[
                pl.BlockSpec(
                    (TOK, 256),
                    lambda kz, kx, at: (0, lax.rem(at[0] + kz, 2) * 4 + lax.rem(at[1] + kx, 4)),
                )
            ],
            out_specs=pl.BlockSpec((1, 1, 4, 64, TOK), lambda kz, kx, at: (kz, kx, 0, 0, 0)),
            scratch_shapes=[pltpu.VMEM((256, TOK), BF16)],
        ),
        out_shape=jax.ShapeDtypeStruct((2, 4, 4, 64, TOK), BF16),
        cost_estimate=pl.CostEstimate(flops=0, bytes_accessed=4 * TOK * D, transcendentals=0),
    )(place, values)


def ring(term, axis):
    ahead = send(term(2, 0), axis, 1)
    behind = send(term(2, 1), axis, -1)
    ahead_one = send(term(1, 1), axis, 1)
    behind_one = send(term(3, 0), axis, -1)
    ahead_sum = send(term(1, 0, ahead), axis, 1)
    behind_sum = send(term(3, 1, behind), axis, -1)
    return term(0, 0, behind_one, ahead_sum), term(0, 1, ahead_one, behind_sum)


def scatter(left, right, first, second):
    def outer(k, h, *more):
        rows = left[h, k] if first == "x" else left[h, :, k]
        total = plain_dot(rows.reshape(256, TOK), right).reshape(4, 64, -1)
        for value in more:
            total = total + value
        return total

    halves = ring(outer, first)

    def inner(k, h, *more):
        total = halves[h][k]
        for value in more:
            total = total + value
        return total

    mine, other = ring(inner, second)
    return mine + send(other, "zl")


def scatter_both(left, right):
    half = right.shape[1] // 2
    return jnp.concatenate(
        [scatter(left, right[:, :half], "x", "y"), scatter(left, right[:, half:], "y", "x")],
        axis=1,
    )


def scatter_small(blocks):
    def outer(k, h, *more):
        total = blocks[h, k]
        for value in more:
            total = total + value
        return total

    halves = ring(outer, "x")

    def inner(k, h, *more):
        total = halves[h][k]
        for value in more:
            total = total + value
        return total

    mine, other = ring(inner, "y")
    return mine + send(other, "zl")


def rolled(blocks, place):
    for axis, at in enumerate(place):
        n = blocks.shape[axis]
        twice = jnp.concatenate([blocks, blocks], axis=axis)
        blocks = lax.dynamic_slice_in_dim(twice, at, n, axis)
    return blocks


def body(
    hidden_in,
    segment_ids,
    positions,
    ln1_gain,
    ln1_bias,
    qkv_weight,
    qkv_bias,
    dense_weight,
    dense_bias,
    ln2_gain,
    ln2_bias,
    fc1_weight,
    fc1_bias,
    fc2_weight,
    fc2_bias,
    cotangent,
):
    place = [lax.axis_index(a) for a in DP]
    where = jnp.stack(place).astype(jnp.int32)
    core = lax.axis_index("c")
    half_rows = TOK // 2

    def of_core(values, which):
        return lax.dynamic_slice_in_dim(values, which * half_rows, half_rows, 0)

    def both_cores(mine):
        theirs = send(mine, "c")
        whole = jnp.zeros((TOK,) + mine.shape[1:], mine.dtype)
        whole = lax.dynamic_update_slice_in_dim(whole, mine, core * half_rows, 0)
        return lax.dynamic_update_slice_in_dim(whole, theirs, (1 - core) * half_rows, 0)

    hidden = hidden_in.astype(F32)
    tokens = TOK
    heads = 2
    cot_rows = turned_rows(cotangent, where)
    average = jnp.mean(hidden, axis=-1, keepdims=True)
    centred = hidden - average
    inv_std = lax.rsqrt(jnp.mean(centred * centred, axis=-1, keepdims=True) + EPSILON)
    normed = centred * inv_std
    first_in = (normed * ln1_gain + ln1_bias).astype(BF16)
    second_in = (normed * ln2_gain + ln2_bias).astype(BF16)

    upward = plain_dot(second_in, fc1_weight) + fc1_bias.reshape(-1)
    act_low = jax.nn.gelu(upward, approximate=False).astype(BF16)
    down_sum = scatter_both(cot_rows, act_low)

    grad_act = contract_cols(cotangent, fc2_weight)
    _, gelu_back = jax.vjp(partial(jax.nn.gelu, approximate=False), upward)
    grad_up = gelu_back(grad_act)[0].astype(BF16)
    second_rows = turned_rows(second_in, where)
    up_sum = scatter_both(second_rows, grad_up)
    up_bias_grad = jnp.sum(grad_up.astype(F32), axis=0)

    packed = (plain_dot(first_in, qkv_weight) + qkv_bias.reshape(-1)).reshape(tokens, heads, 3, HD)
    cosine, sine = angle_tables(positions)
    cosine = cosine[:, None, :]
    sine = sine[:, None, :]
    queries = rotate(packed[:, :, 0], cosine, sine).astype(BF16)
    keys_rot = rotate(packed[:, :, 1], cosine, sine).astype(BF16)
    values_in = packed[:, :, 2].astype(BF16)
    scores = masked_scores(queries, keys_rot, segment_ids)
    top = jnp.max(scores, axis=-1, keepdims=True)
    weights = jnp.exp(scores - top)
    totals = jnp.sum(weights, axis=-1, keepdims=True)
    probs = weights / totals
    probs_low = probs.astype(BF16)
    mixed = jnp.einsum("hqk,khd->qhd", probs_low, values_in, preferred_element_type=F32)
    mixed_low = mixed.reshape(tokens, heads * HD).astype(BF16)

    grad_mixed = contract_cols(cotangent, dense_weight).astype(BF16).reshape(tokens, heads, HD)
    grad_probs = jnp.einsum("qhd,khd->hqk", grad_mixed, values_in, preferred_element_type=F32)
    along = jnp.sum(probs * grad_probs, axis=-1, keepdims=True)
    grad_scores = (probs * (grad_probs - along)).astype(BF16)
    score_scale = 1.0 / math.sqrt(HD)
    grad_query = (
        jnp.einsum("hqk,khd->qhd", grad_scores, keys_rot, preferred_element_type=F32) * score_scale
    )
    grad_key = (
        jnp.einsum("hqk,qhd->khd", grad_scores, queries, preferred_element_type=F32) * score_scale
    )
    grad_value = jnp.einsum("hqk,qhd->khd", probs_low, grad_mixed, preferred_element_type=F32)
    grad_packed = jnp.stack(
        [rotate(grad_query, cosine, -sine), rotate(grad_key, cosine, -sine), grad_value], axis=2
    )
    grad_packed = grad_packed.reshape(tokens, heads * 3 * HD).astype(BF16)
    first_rows = turned_rows(first_in, where)
    dense_sum = scatter_both(cot_rows, mixed_low)
    qkv_sum = scatter_both(first_rows, grad_packed)
    qkv_bias_sum = jnp.sum(grad_packed.astype(F32), axis=0)

    def branch_half(which):
        return plain_dot(of_core(mixed_low, which), dense_weight) + plain_dot(
            of_core(act_low, which), fc2_weight
        )

    branch = branch_half(core) + send(branch_half(1 - core), "c")
    branch = branch + send(branch, "zh")
    output = both_cores(of_core(hidden, core) + branch + dense_bias + fc2_bias)

    first_part = contract_cols(grad_packed, qkv_weight)
    second_part = contract_cols(grad_up, fc1_weight)
    combined = first_part * ln1_gain + second_part * ln2_gain
    combined = of_core(combined, core) + send(of_core(combined, 1 - core), "c")
    combined = combined + send(combined, "zh")
    normed_half = of_core(normed, core)
    grad_out = cotangent.astype(F32)
    input_half = of_core(grad_out, core) + of_core(inv_std, core) * (
        combined
        - jnp.mean(combined, axis=-1, keepdims=True)
        - normed_half * jnp.mean(combined * normed_half, axis=-1, keepdims=True)
    )
    input_grad = both_cores(input_half)

    gain_one_grad = jnp.sum(first_part * normed, axis=0)
    shift_one_grad = jnp.sum(first_part, axis=0)
    gain_two_grad = jnp.sum(second_part * normed, axis=0)
    shift_two_grad = jnp.sum(second_part, axis=0)
    bias_sum = jnp.sum(grad_out, axis=0)
    features = jnp.stack(
        [gain_one_grad, shift_one_grad, gain_two_grad, shift_two_grad, bias_sum]
    ).reshape(5, 32, 64)
    small = jnp.concatenate(
        [
            features.transpose(1, 0, 2).reshape(32, 320),
            qkv_bias_sum.reshape(2, 32, 24).transpose(1, 0, 2).reshape(32, 48),
            up_bias_grad.reshape(16, 32, 4).transpose(1, 0, 2).reshape(32, 64),
            jnp.zeros((32, 80), F32),
        ],
        axis=1,
    )
    small = rolled(small.reshape(2, 4, 4, 512), place)
    small = scatter_small(small)
    norms = small[:256]
    norms = norms + send(norms, "c")
    norms = (norms + send(norms, "zh")).reshape(4, 64)
    bias_total = small[256:320]
    return (
        output,
        input_grad,
        norms[0],
        norms[1],
        qkv_sum,
        small[320:368].reshape(2, 24),
        dense_sum.T,
        bias_total,
        norms[2],
        norms[3],
        up_sum,
        small[368:432].reshape(16, 4),
        down_sum.T,
        bias_total,
    )


def solution(mesh):
    fine = Mesh(mesh.devices.reshape(tuple(SIZES.values())), tuple(SIZES))
    return jax.shard_map(
        body,
        mesh=fine,
        in_specs=(
            P(DP, None),
            P(DP),
            P(DP),
            P(),
            P(),
            P(None, TENSOR),
            P(TENSOR, None),
            P(TENSOR, None),
            P(),
            P(),
            P(),
            P(None, TENSOR),
            P(TENSOR, None),
            P(TENSOR, None),
            P(),
            P(DP, None),
        ),
        out_specs=(
            P(DP, None),
            P(DP, None),
            P(DP),
            P(DP),
            P(DP, TENSOR),
            P(TENSOR, DP),
            P(TENSOR, DP),
            P(DP),
            P(DP),
            P(DP),
            P(DP, TENSOR),
            P(TENSOR, DP),
            P(TENSOR, DP),
            P(DP),
        ),
        check_vma=False,
    )
```

time: 891 us -> 717 us (0.80); the launches traced: 887 us -> 703 us
  waiting for transfers between devices: 560 us -> 276 us
  starting transfers between devices: 0.43 us -> 172 us
  blocking collectives: 158 us -> 0 us
  matrix products: 103 us -> 142 us
  Pallas kernels: 0 us -> 29.4 us
  other arithmetic: 24.5 us -> 42.9 us
  between operations: 18.4 us -> 2.9 us
  local copies, waits for them, and re-layouts: 23.2 us -> 37.6 us
    psum x1 -> x0, waiting for transfers between devices: 532 us -> none  [body(): branches = lax.psum(attn_part, 'tensor') + lax.psum(mlp_part, 'tensor')]
    ppermute x0 -> x125, waiting for transfers between devices: none -> 276 us  [send(): return lax.ppermute(value, axis, [(i, (i + step) % n) for i in range(n)])]
    ppermute x0 -> x125, starting transfers between devices: none -> 172 us  [send(): return lax.ppermute(value, axis, [(i, (i + step) % n) for i in range(n)])]
    unnamed x1 -> x0, blocking collectives: 158 us -> none
    pallas_call x0 -> x3, Pallas kernels: none -> 29.4 us  [turned_rows(): pl.pallas_call(turn_kernel, grid_spec=pltpu.PrefetchScalarGridSpec(num_sc...]
    dot_general x11 -> x72, matrix products: 66.4 us -> 95.7 us  [the longest x70 92.7 us: plain_dot(): return jnp.dot(left, right, preferred_element_type=F32)]
    reduce_scatter x4 -> x0, waiting for transfers between devices: 27 us -> none  [the longest x1 27 us: body(): lax.psum_scatter(down_grad, 'dp', scatter_dimension=1, tiled=True)]
    convert_element_type x3 -> x6, other arithmetic: 1.79 us -> 14.8 us  [the longest x1 4.61 us: body(): act_low = jax.nn.gelu(upward, approximate=False).astype(BF16)]
  transfers between devices with their start and end apart: 5 -> 125, of which waited for: 2 -> 48; matrix products, arithmetic and copies ran while one was open for 6% -> 24% of each run, Pallas kernels for 0% -> 3%
where the time goes in v1:
time: 717 us; the launch traced here: 703 us
  waiting for transfers between devices  276 us (38%)
  starting transfers between devices  172 us (24%)
  matrix products  142 us (20%)
  other arithmetic  42.9 us (6%)
  local copies, waits for them, and re-layouts  37.6 us (5%)
  Pallas kernels  29.4 us (4%)
    ppermute x125, waiting for transfers between devices, send(): return lax.ppermute(value, axis, [(i, (i + step) % n) for i in range(n)])  276 us
    ppermute x125, starting transfers between devices, send(): return lax.ppermute(value, axis, [(i, (i + step) % n) for i in range(n)])  172 us
    dot_general x70, matrix products, plain_dot(): return jnp.dot(left, right, preferred_element_type=F32)  92.7 us
    dot_general x4, matrix products, contract_cols(): lax.dot_general(left, right, (((1,), (1,)), ((), ())), preferred_element_...  38.3 us
    pallas_call x3, Pallas kernels, turned_rows(): pl.pallas_call(turn_kernel, grid_spec=pltpu.PrefetchScalarGridSpec(num_sc...  29.4 us
    unnamed x168, local copies, waits for them, and re-layouts  17.4 us
  transfers between devices with their start and end apart: 125, of which 48 were waited for; matrix products, arithmetic and copies ran while one was open for 24% of the time, Pallas kernels for 3%

profile of v1, /device:TPU:0, one launch (start us, length us, event | category | flops | bytes accessed | tf_op | source)
XLA Modules:
  0.0 703.4 jit_solution(9762337773447822686)
XLA Ops:
  3.8 4.5 add_convert_fusion.2
  9.7 5.1 convolution_add_fusion
  35.0 6.9 shard_map.264
  44.7 3.9 fusion.176
  77.1 8.9 %fusion.178 = f32[512,2048]{1,0:T(8,128)} fusion(bf16[512,1536]{0,1:T(8,128)(2,1)} %bitcast.605, bf16[2048,1536]{1,0:T(8,128)(2,1)} %param.21), kind=kOutput, calls=%fused_computation.426 | convolution fusion | flops 3221225472 | bytes 12058624 | tf_op jit(solution)/shard_map/dot_general | solution.py:50
  86.0 7.0 %fusion.177 = f32[512,2048]{1,0:T(8,128)S(1)} fusion(bf16[512,2048]{1,0:T(8,128)(2,1)S(1)} %copy-done.26, bf16[2048,2048]{1,0:T(8,128)(2,1)} %param.27), kind=kOutput, calls=%fused_computation.425 | convolution fusion | flops 4294967296 | bytes 14680064 | tf_op jit(solution)/shard_map/dot_general | solution.py:46
  93.2 15.4 %convert_reduce_fusion = (f32[2048]{0:T(1024)S(1)}, bf16[512,2048]{1,0:T(8,128)(2,1)S(1)}, f32[512,2048]{1,0:T(8,128)}) fusion(f32[512,2048]{1,0:T(8,128)S(1)} %fusion.177, f32[2048]{0:T(1024)S(1)} %bitcast.656, bf16[512,2048]{1,0:T(8,128)(2,1)S(1)} %copy-done.15, bf16[2048,2048]{1,0:T(8,128)(2,1)S(1)} %bitcast.663), kind=kOutput, calls=%fused_computation.3 | convolution fusion | flops 4373608448 | bytes 20987904 | tf_op jit(solution)/shard_map/dot_general | solution.py:50
  108.6 12.7 %fusion.167 = (f32[2048]{0:T(1024)S(1)}, f32[2048]{0:T(1024)S(1)}, f32[512,2048]{1,0:T(8,128)}, f32[2048]{0:T(1024)S(1)}, f32[2048]{0:T(1024)S(1)}, /*index=5*/f32[512,2048]{1,0:T(8,128)}) fusion(f32[512]{0:T(512)S(1)} %add_rsqrt_fusion, f32[512]{0:T(512)S(1)} %broadcast_multiply_fusion.1, bf16[512,2048]{1,0:T(8,128)(2,1)S(1)} %copy-done.12, ...), kind=kOutput, calls=%fused_computation.416 | convolution fusion | flops 4307542016 | bytes 25219072 | tf_op jit(solution)/shard_map/dot_general | solution.py:50
  126.9 4.6 multiply_convert_fusion
  143.2 15.7 %shard_map.265 = bf16[2,4,4,64,512]{4,3,2,1,0:T(8,128)(2,1)} custom-call(s32[3]{0:T(128)} %pad_add_fusion.place, bf16[512,2048]{1,0:T(8,128)(2,1)} %get-tuple-element.79.source), custom_call_target="tpu_custom_call" | custom-call | bytes 4194304 | tf_op jit(solution)/shard_map/pallas_call | solution.py:70
  172.7 6.9 shard_map.263
  191.8 6.2 fusion.27
  201.7 7.5 %fusion.29 = f32[256,2048]{1,0:T(8,128)} fusion(bf16[2048,2048]{1,0:T(8,128)(2,1)} %param.29, bf16[512,2048]{1,0:T(8,128)(2,1)} %copy-done.1, s32[]{:T(128)S(6)} %select_n.14), kind=kOutput, calls=%fused_computation.109 | convolution fusion | flops 2147483648 | bytes 11534340 | tf_op jit(solution)/shard_map/dot_general | solution.py:46
  257.0 5.2 collective-permute-done.67
  289.4 5.5 collective-permute-done.64
  294.9 4.2 collective-permute-done.70
  325.7 16.3 %collective-permute-done.35 = f32[4,64,768]{2,1,0:T(8,128)S(1)} collective-permute-done((f32[4,64,768]{2,1,0:T(8,128)S(1)}, f32[4,64,768]{2,1,0:T(8,128)S(1)}, u32[]{:S(2)}, u32[]{:S(2)}) %collective-permute-start.35) | collective-permute-done | bytes 786464 | tf_op jit(solution)/shard_map/ppermute | solution.py:26
  351.6 12.3 %collective-permute-done.119 = f32[4,64,1024]{2,1,0:T(8,128)S(1)} collective-permute-done((f32[4,64,1024]{2,1,0:T(8,128)S(1)}, f32[4,64,1024]{2,1,0:T(8,128)S(1)}, u32[]{:S(2)}, u32[]{:S(2)}) %collective-permute-start.119) | collective-permute-done | bytes 1048608 | tf_op jit(solution)/shard_map/ppermute | solution.py:26
  373.3 6.4 collective-permute-done.93
  388.3 19.1 %collective-permute-done.23 = f32[4,64,768]{2,1,0:T(8,128)S(1)} collective-permute-done((f32[4,64,768]{2,1,0:T(8,128)S(1)}, f32[4,64,768]{2,1,0:T(8,128)S(1)}, u32[]{:S(2)}, u32[]{:S(2)}) %collective-permute-start.23) | collective-permute-done | bytes 786464 | tf_op jit(solution)/shard_map/ppermute | solution.py:26
  412.3 27.8 %collective-permute-done.36 = f32[4,64,768]{2,1,0:T(8,128)S(1)} collective-permute-done((f32[4,64,768]{2,1,0:T(8,128)S(1)}, f32[4,64,768]{2,1,0:T(8,128)S(1)}, u32[]{:S(2)}, u32[]{:S(2)}) %collective-permute-start.36) | collective-permute-done | bytes 786464 | tf_op jit(solution)/shard_map/ppermute | solution.py:26
  451.2 7.0 collective-permute-done.38
  461.3 4.8 collective-permute-done.44
  469.8 16.6 %collective-permute-done.43 = f32[64,768]{1,0:T(8,128)S(1)} collective-permute-done((f32[64,768]{1,0:T(8,128)S(1)}, f32[64,768]{1,0:T(8,128)S(1)}, u32[]{:S(2)}, u32[]{:S(2)}) %collective-permute-start.43) | collective-permute-done | bytes 196640 | tf_op jit(solution)/shard_map/ppermute | solution.py:26
  486.4 3.9 collective-permute-start.120
  505.3 8.6 %collective-permute-done.112 = f32[4,64,1024]{2,1,0:T(8,128)S(1)} collective-permute-done((f32[4,64,1024]{2,1,0:T(8,128)S(1)}, f32[4,64,1024]{2,1,0:T(8,128)S(1)}, u32[]{:S(2)}, u32[]{:S(2)}) %collective-permute-start.112) | collective-permute-done | bytes 1048608 | tf_op jit(solution)/shard_map/ppermute | solution.py:26
  520.7 6.5 collective-permute-done.73
  527.2 4.3 collective-permute-done.75
  534.5 21.0 %collective-permute-done.94 = f32[4,64,1024]{2,1,0:T(8,128)S(1)} collective-permute-done((f32[4,64,1024]{2,1,0:T(8,128)S(1)}, f32[4,64,1024]{2,1,0:T(8,128)S(1)}, u32[]{:S(2)}, u32[]{:S(2)}) %collective-permute-start.94) | collective-permute-done | bytes 1048608 | tf_op jit(solution)/shard_map/ppermute | solution.py:26
  574.5 5.1 collective-permute-done.103
  609.9 19.8 %collective-permute-done.4 = f32[256,2048]{1,0:T(8,128)S(1)} collective-permute-done((f32[256,2048]{1,0:T(8,128)S(1)}, f32[256,2048]{1,0:T(8,128)S(1)}, u32[]{:S(2)}, u32[]{:S(2)}) %collective-permute-start.4) | collective-permute-done | bytes 2097184 | tf_op jit(solution)/shard_map/ppermute | solution.py:26
  639.7 29.1 %collective-permute-done.1 = f32[256,2048]{1,0:T(8,128)S(1)} collective-permute-done((f32[256,2048]{1,0:T(8,128)S(1)}, f32[256,2048]{1,0:T(8,128)S(1)}, u32[]{:S(2)}, u32[]{:S(2)}) %collective-permute-start.1) | collective-permute-done | bytes 2097184 | tf_op jit(solution)/shard_map/ppermute | solution.py:26
  (602 shorter events, 371.8 us)
Async XLA Ops:
  53.1 194.3 %collective-permute-start.48 = (f32[4,64,256]{2,1,0:T(8,128)}, f32[4,64,256]{2,1,0:T(8,128)}, u32[]{:S(2)}, u32[]{:S(2)}) collective-permute-start(f32[4,64,256]{2,1,0:T(8,128)} %fusion.93), channel_id=1, source_target_pairs={{0,16},{16,32},{32,48},{48,0},{1,17},{17,33},{33,49},{49,1},{2,18}... | collective-permute-start | bytes 786440 | tf_op jit(solution)/shard_map/ppermute | solution.py:26
  56.6 206.4 %collective-permute-start.47 = (f32[4,64,256]{2,1,0:T(8,128)}, f32[4,64,256]{2,1,0:T(8,128)}, u32[]{:S(2)}, u32[]{:S(2)}) collective-permute-start(f32[4,64,256]{2,1,0:T(8,128)} %fusion.91), channel_id=1, source_target_pairs={{0,48},{16,0},{32,16},{48,32},{1,49},{17,1},{33,17},{49,33},{2,50}... | collective-permute-start | bytes 786440 | tf_op jit(solution)/shard_map/ppermute | solution.py:26
  123.2 87.0 %collective-permute-start.7 = (f32[4,512]{1,0:T(4,128)S(1)}, f32[4,512]{1,0:T(4,128)S(1)}, u32[]{:S(2)}, u32[]{:S(2)}) collective-permute-start(f32[4,512]{1,0:T(4,128)S(1)} %get-tuple-element.131), channel_id=1, source_target_pairs={{0,16},{16,32},{32,48},{48,0},{1,17},{17,33},{33,49},{49,1},{2,18}... | collective-permute-start | bytes 24584 | tf_op jit(solution)/shard_map/ppermute | solution.py:26
  123.6 89.3 %collective-permute-start.13 = (f32[4,512]{1,0:T(4,128)S(1)}, f32[4,512]{1,0:T(4,128)S(1)}, u32[]{:S(2)}, u32[]{:S(2)}) collective-permute-start(f32[4,512]{1,0:T(4,128)S(1)} %get-tuple-element.132), channel_id=1, source_target_pairs={{0,48},{16,0},{32,16},{48,32},{1,49},{17,1},{33,17},{49,33},{2,50}... | collective-permute-start | bytes 24584 | tf_op jit(solution)/shard_map/ppermute | solution.py:26
  126.5 86.4 %collective-permute-start.6 = (f32[4,512]{1,0:T(4,128)S(1)}, f32[4,512]{1,0:T(4,128)S(1)}, u32[]{:S(2)}, u32[]{:S(2)}) collective-permute-start(f32[4,512]{1,0:T(4,128)S(1)} %get-tuple-element.129), channel_id=1, source_target_pairs={{0,48},{16,0},{32,16},{48,32},{1,49},{17,1},{33,17},{49,33},{2,50}... | collective-permute-start | bytes 24584 | tf_op jit(solution)/shard_map/ppermute | solution.py:26
  235.3 34.1 %collective-permute-start.53 = (f32[4,64,256]{2,1,0:T(8,128)}, f32[4,64,256]{2,1,0:T(8,128)}, u32[]{:S(2)}, u32[]{:S(2)}) collective-permute-start(f32[4,64,256]{2,1,0:T(8,128)} %fusion.95), channel_id=1, source_target_pairs={{0,16},{16,32},{32,48},{48,0},{1,17},{17,33},{33,49},{49,1},{2,18}... | collective-permute-start | bytes 786440 | tf_op jit(solution)/shard_map/ppermute | solution.py:26
  269.4 52.0 %collective-permute-start.22 = (f32[4,64,768]{2,1,0:T(8,128)S(1)}, f32[4,64,768]{2,1,0:T(8,128)S(1)}, u32[]{:S(2)}, u32[]{:S(2)}) collective-permute-start(f32[4,64,768]{2,1,0:T(8,128)S(1)} %copy-done.64), channel_id=1, source_target_pairs={{0,16},{16,32},{32,48},{48,0},{1,17},{17,33},{33,49},{49,1},{2,18}... | collective-permute-start | bytes 2359304 | tf_op jit(solution)/shard_map/ppermute | solution.py:26
  271.2 54.0 %collective-permute-start.28 = (f32[4,64,768]{2,1,0:T(8,128)S(1)}, f32[4,64,768]{2,1,0:T(8,128)S(1)}, u32[]{:S(2)}, u32[]{:S(2)}) collective-permute-start(f32[4,64,768]{2,1,0:T(8,128)S(1)} %copy-done.63), channel_id=1, source_target_pairs={{0,48},{16,0},{32,16},{48,32},{1,49},{17,1},{33,17},{49,33},{2,50}... | collective-permute-start | bytes 2359304 | tf_op jit(solution)/shard_map/ppermute | solution.py:26
  314.7 31.7 %collective-permute-start.106 = (f32[4,64,1024]{2,1,0:T(8,128)S(1)}, f32[4,64,1024]{2,1,0:T(8,128)S(1)}, u32[]{:S(2)}, u32[]{:S(2)}) collective-permute-start(f32[4,64,1024]{2,1,0:T(8,128)S(1)} %copy-done.55), channel_id=1, source_target_pairs={{0,48},{16,0},{32,16},{48,32},{1,49},{17,1},{33,17},{49,33},{2,50}... | collective-permute-start | bytes 3145736 | tf_op jit(solution)/shard_map/ppermute | solution.py:26
  325.1 38.8 %collective-permute-start.119 = (f32[4,64,1024]{2,1,0:T(8,128)S(1)}, f32[4,64,1024]{2,1,0:T(8,128)S(1)}, u32[]{:S(2)}, u32[]{:S(2)}) collective-permute-start(f32[4,64,1024]{2,1,0:T(8,128)S(1)} %copy-done.53), channel_id=1, source_target_pairs={{0,12},{4,0},{8,4},{12,8},{1,13},{5,1},{9,5},{13,9},{2,14},{6,2},{... | collective-permute-start | bytes 3145736 | tf_op jit(solution)/shard_map/ppermute | solution.py:26
  347.6 32.1 %collective-permute-start.93 = (f32[4,64,1024]{2,1,0:T(8,128)S(1)}, f32[4,64,1024]{2,1,0:T(8,128)S(1)}, u32[]{:S(2)}, u32[]{:S(2)}) collective-permute-start(f32[4,64,1024]{2,1,0:T(8,128)S(1)} %copy-done.49), channel_id=1, source_target_pairs={{0,12},{4,0},{8,4},{12,8},{1,13},{5,1},{9,5},{13,9},{2,14},{6,2},{... | collective-permute-start | bytes 3145736 | tf_op jit(solution)/shard_map/ppermute | solution.py:26
  371.2 36.7 %collective-permute-start.27 = (f32[4,64,768]{2,1,0:T(8,128)S(1)}, f32[4,64,768]{2,1,0:T(8,128)S(1)}, u32[]{:S(2)}, u32[]{:S(2)}) collective-permute-start(f32[4,64,768]{2,1,0:T(8,128)S(1)} %copy-done.59), channel_id=1, source_target_pairs={{0,16},{16,32},{32,48},{48,0},{1,17},{17,33},{33,49},{49,1},{2,18}... | collective-permute-start | bytes 2359304 | tf_op jit(solution)/shard_map/ppermute | solution.py:26
  372.9 34.6 %collective-permute-start.23 = (f32[4,64,768]{2,1,0:T(8,128)S(1)}, f32[4,64,768]{2,1,0:T(8,128)S(1)}, u32[]{:S(2)}, u32[]{:S(2)}) collective-permute-start(f32[4,64,768]{2,1,0:T(8,128)S(1)} %convolution_add_fusion.25), channel_id=1, source_target_pairs={{0,16},{16,32},{32,48},{48,0},{1,17},{17,33},{33,49},{49,1},{2,18}... | collective-permute-start | bytes 2359304 | tf_op jit(solution)/shard_map/ppermute | solution.py:26
  383.5 74.7 %collective-permute-start.105 = (f32[4,64,1024]{2,1,0:T(8,128)S(1)}, f32[4,64,1024]{2,1,0:T(8,128)S(1)}, u32[]{:S(2)}, u32[]{:S(2)}) collective-permute-start(f32[4,64,1024]{2,1,0:T(8,128)S(1)} %copy-done.47), channel_id=1, source_target_pairs={{0,16},{16,32},{32,48},{48,0},{1,17},{17,33},{33,49},{49,1},{2,18}... | collective-permute-start | bytes 3145736 | tf_op jit(solution)/shard_map/ppermute | solution.py:26
  407.4 33.0 %collective-permute-start.40 = (f32[4,64,768]{2,1,0:T(8,128)S(1)}, f32[4,64,768]{2,1,0:T(8,128)S(1)}, u32[]{:S(2)}, u32[]{:S(2)}) collective-permute-start(f32[4,64,768]{2,1,0:T(8,128)S(1)} %fusion.81), channel_id=1, source_target_pairs={{0,4},{4,8},{8,12},{12,0},{1,5},{5,9},{9,13},{13,1},{2,6},{6,10},{... | collective-permute-start | bytes 2359304 | tf_op jit(solution)/shard_map/ppermute | solution.py:26
  407.9 32.2 %collective-permute-start.36 = (f32[4,64,768]{2,1,0:T(8,128)S(1)}, f32[4,64,768]{2,1,0:T(8,128)S(1)}, u32[]{:S(2)}, u32[]{:S(2)}) collective-permute-start(f32[4,64,768]{2,1,0:T(8,128)S(1)} %convolution_add_fusion.21), channel_id=1, source_target_pairs={{0,4},{4,8},{8,12},{12,0},{1,5},{5,9},{9,13},{13,1},{2,6},{6,10},{... | collective-permute-start | bytes 2359304 | tf_op jit(solution)/shard_map/ppermute | solution.py:26
  409.6 31.0 %collective-permute-start.42 = (f32[4,64,768]{2,1,0:T(8,128)S(1)}, f32[4,64,768]{2,1,0:T(8,128)S(1)}, u32[]{:S(2)}, u32[]{:S(2)}) collective-permute-start(f32[4,64,768]{2,1,0:T(8,128)S(1)} %convolution_add_fusion.19), channel_id=1, source_target_pairs={{0,12},{4,0},{8,4},{12,8},{1,13},{5,1},{9,5},{13,9},{2,14},{6,2},{... | collective-permute-start | bytes 2359304 | tf_op jit(solution)/shard_map/ppermute | solution.py:26
  412.2 46.2 %collective-permute-start.99 = (f32[4,64,1024]{2,1,0:T(8,128)S(1)}, f32[4,64,1024]{2,1,0:T(8,128)S(1)}, u32[]{:S(2)}, u32[]{:S(2)}) collective-permute-start(f32[4,64,1024]{2,1,0:T(8,128)S(1)} %copy-done.46), channel_id=1, source_target_pairs={{0,48},{16,0},{32,16},{48,32},{1,49},{17,1},{33,17},{49,33},{2,50}... | collective-permute-start | bytes 3145736 | tf_op jit(solution)/shard_map/ppermute | solution.py:26
  440.1 57.8 %collective-permute-start.107 = (f32[4,64,1024]{2,1,0:T(8,128)S(1)}, f32[4,64,1024]{2,1,0:T(8,128)S(1)}, u32[]{:S(2)}, u32[]{:S(2)}) collective-permute-start(f32[4,64,1024]{2,1,0:T(8,128)S(1)} %convolution_add_fusion.7), channel_id=1, source_target_pairs={{0,48},{16,0},{32,16},{48,32},{1,49},{17,1},{33,17},{49,33},{2,50}... | collective-permute-start | bytes 3145736 | tf_op jit(solution)/shard_map/ppermute | solution.py:26
  458.2 40.3 %collective-permute-start.118 = (f32[4,64,1024]{2,1,0:T(8,128)S(1)}, f32[4,64,1024]{2,1,0:T(8,128)S(1)}, u32[]{:S(2)}, u32[]{:S(2)}) collective-permute-start(f32[4,64,1024]{2,1,0:T(8,128)S(1)} %copy-done.45), channel_id=1, source_target_pairs={{0,4},{4,8},{8,12},{12,0},{1,5},{5,9},{9,13},{13,1},{2,6},{6,10},{... | collective-permute-start | bytes 3145736 | tf_op jit(solution)/shard_map/ppermute | solution.py:26
  458.3 42.8 %collective-permute-start.101 = (f32[4,64,1024]{2,1,0:T(8,128)S(1)}, f32[4,64,1024]{2,1,0:T(8,128)S(1)}, u32[]{:S(2)}, u32[]{:S(2)}) collective-permute-start(f32[4,64,1024]{2,1,0:T(8,128)S(1)} %convolution_add_fusion.9), channel_id=1, source_target_pairs={{0,16},{16,32},{32,48},{48,0},{1,17},{17,33},{33,49},{49,1},{2,18}... | collective-permute-start | bytes 3145736 | tf_op jit(solution)/shard_map/ppermute | solution.py:26
  518.1 40.9 %collective-permute-start.86 = (f32[4,64,1024]{2,1,0:T(8,128)S(1)}, f32[4,64,1024]{2,1,0:T(8,128)S(1)}, u32[]{:S(2)}, u32[]{:S(2)}) collective-permute-start(f32[4,64,1024]{2,1,0:T(8,128)S(1)} %copy-done.40), channel_id=1, source_target_pairs={{0,12},{4,0},{8,4},{12,8},{1,13},{5,1},{9,5},{13,9},{2,14},{6,2},{... | collective-permute-start | bytes 3145736 | tf_op jit(solution)/shard_map/ppermute | solution.py:26
  520.1 40.9 %collective-permute-start.3 = (f32[256,2048]{1,0:T(8,128)S(1)}, f32[256,2048]{1,0:T(8,128)S(1)}, u32[]{:S(2)}, u32[]{:S(2)}) collective-permute-start(f32[256,2048]{1,0:T(8,128)S(1)} %copy-done.36), channel_id=1, source_target_pairs={{0,1},{1,0},{2,3},{3,2},{4,5},{5,4},{6,7},{7,6},{8,9},{9,8},{10,11... | collective-permute-start | bytes 6291464 | tf_op jit(solution)/shard_map/ppermute | solution.py:26
  527.2 34.9 %collective-permute-start = (f32[256,2048]{1,0:T(8,128)S(1)}, f32[256,2048]{1,0:T(8,128)S(1)}, u32[]{:S(2)}, u32[]{:S(2)}) collective-permute-start(f32[256,2048]{1,0:T(8,128)S(1)} %copy-done.35), channel_id=1, source_target_pairs={{0,1},{1,0},{2,3},{3,2},{4,5},{5,4},{6,7},{7,6},{8,9},{9,8},{10,11... | collective-permute-start | bytes 6291464 | tf_op jit(solution)/shard_map/ppermute | solution.py:26
  573.2 32.9 %collective-permute-start.121 = (f32[64,1024]{1,0:T(8,128)S(1)}, f32[64,1024]{1,0:T(8,128)S(1)}, u32[]{:S(2)}, u32[]{:S(2)}) collective-permute-start(f32[64,1024]{1,0:T(8,128)S(1)} %get-tuple-element.86), channel_id=1, source_target_pairs={{0,16},{16,32},{32,48},{48,0},{1,17},{17,33},{33,49},{49,1},{2,18}... | collective-permute-start | bytes 786440 | tf_op jit(solution)/shard_map/ppermute | solution.py:26
  579.6 50.1 %collective-permute-start.4 = (f32[256,2048]{1,0:T(8,128)S(1)}, f32[256,2048]{1,0:T(8,128)S(1)}, u32[]{:S(2)}, u32[]{:S(2)}) collective-permute-start(f32[256,2048]{1,0:T(8,128)S(1)} %dynamic-slice_add_fusion), channel_id=1, source_target_pairs={{0,2},{2,0},{1,3},{3,1},{4,6},{6,4},{5,7},{7,5},{8,10},{10,8},{9,1... | collective-permute-start | bytes 6291464 | tf_op jit(solution)/shard_map/ppermute | solution.py:26
  598.5 70.3 %collective-permute-start.1 = (f32[256,2048]{1,0:T(8,128)S(1)}, f32[256,2048]{1,0:T(8,128)S(1)}, u32[]{:S(2)}, u32[]{:S(2)}) collective-permute-start(f32[256,2048]{1,0:T(8,128)S(1)} %fusion.7), channel_id=1, source_target_pairs={{0,2},{2,0},{1,3},{3,1},{4,6},{6,4},{5,7},{7,5},{8,10},{10,8},{9,1... | collective-permute-start | bytes 6291464 | tf_op jit(solution)/shard_map/ppermute | solution.py:26
  629.7 42.2 %collective-permute-start.95 = (f32[64,1024]{1,0:T(8,128)S(1)}, f32[64,1024]{1,0:T(8,128)}, u32[]{:S(2)}, u32[]{:S(2)}) collective-permute-start(f32[64,1024]{1,0:T(8,128)S(1)} %get-tuple-element.94), channel_id=1, source_target_pairs={{0,16},{16,32},{32,48},{48,0},{1,17},{17,33},{33,49},{49,1},{2,18}... | collective-permute-start | bytes 786440 | tf_op jit(solution)/shard_map/ppermute | solution.py:26
  633.3 38.7 %collective-permute-start.104 = (f32[64,1024]{1,0:T(8,128)S(1)}, f32[64,1024]{1,0:T(8,128)S(1)}, u32[]{:S(2)}, u32[]{:S(2)}) collective-permute-start(f32[64,1024]{1,0:T(8,128)S(1)} %fusion.54), channel_id=1, source_target_pairs={{0,4},{4,8},{8,12},{12,0},{1,5},{5,9},{9,13},{13,1},{2,6},{6,10},{... | collective-permute-start | bytes 786440 | tf_op jit(solution)/shard_map/ppermute | solution.py:26
  633.4 40.8 %collective-permute-start.84 = (f32[64,1024]{1,0:T(8,128)S(1)}, f32[64,1024]{1,0:T(8,128)}, u32[]{:S(2)}, u32[]{:S(2)}) collective-permute-start(f32[64,1024]{1,0:T(8,128)S(1)} %fusion.69), channel_id=1, source_target_pairs={{0,12},{4,0},{8,4},{12,8},{1,13},{5,1},{9,5},{13,9},{2,14},{6,2},{... | collective-permute-start | bytes 786440 | tf_op jit(solution)/shard_map/ppermute | solution.py:26
  636.6 37.7 %collective-permute-start.97 = (f32[64,1024]{1,0:T(8,128)S(1)}, f32[64,1024]{1,0:T(8,128)}, u32[]{:S(2)}, u32[]{:S(2)}) collective-permute-start(f32[64,1024]{1,0:T(8,128)S(1)} %fusion.58), channel_id=1, source_target_pairs={{0,48},{16,0},{32,16},{48,32},{1,49},{17,1},{33,17},{49,33},{2,50}... | collective-permute-start | bytes 786440 | tf_op jit(solution)/shard_map/ppermute | solution.py:26
  668.8 30.1 %collective-permute-start.5 = (f32[256,2048]{1,0:T(8,128)S(1)}, f32[256,2048]{1,0:T(8,128)S(1)}, u32[]{:S(2)}, u32[]{:S(2)}) collective-permute-start(f32[256,2048]{1,0:T(8,128)S(1)} %get-tuple-element.68), channel_id=1, source_target_pairs={{0,1},{1,0},{2,3},{3,2},{4,5},{5,4},{6,7},{7,6},{8,9},{9,8},{10,11... | collective-permute-start | bytes 6291464 | tf_op jit(solution)/shard_map/ppermute | solution.py:26
  (175 other events, 2714.0 us)

commit v2 on v1

v2 whole, which is shorter than its diff:
```python
from functools import partial
import math

import jax
import jax.numpy as jnp
from jax import lax
from jax.experimental import pallas as pl
from jax.sharding import Mesh, PartitionSpec as P

HD = 256
ROT = 64
TOK = 512
D = 2048
EPSILON = 1e-05
NEGATIVE = -1000000000.0
SIZES = {"zl": 2, "x": 4, "y": 4, "zh": 2, "c": 2}
DP = ("zl", "x", "y")
TENSOR = ("zh", "c")
F32 = jnp.float32
BF16 = jnp.bfloat16


def send(value, axis, step=1):
    n = SIZES[axis]
    return lax.ppermute(value, axis, [(i, (i + step) % n) for i in range(n)])


def angle_tables(positions):
    halves = jnp.arange(ROT // 2, dtype=F32)
    inverse = 10000.0 ** (-2.0 * halves / ROT)
    angles = positions.astype(F32)[..., None] * inverse
    angles = jnp.concatenate([angles, angles], axis=-1)
    return (jnp.cos(angles), jnp.sin(angles))


def rotate(vectors, cosine, sine):
    turned = vectors[..., :ROT]
    first = turned[..., : ROT // 2]
    second = turned[..., ROT // 2 :]
    swapped = jnp.concatenate([-second, first], axis=-1)
    return jnp.concatenate([turned * cosine + swapped * sine, vectors[..., ROT:]], axis=-1)


def plain_dot(left, right):
    return jnp.dot(left, right, preferred_element_type=F32)


def contract_cols(left, right):
    return lax.dot_general(left, right, (((1,), (1,)), ((), ())), preferred_element_type=F32)


def turn_kernel(source, *targets):
    rows = source[...].astype(F32)
    targets[0][0, :, 0] = rows.T.astype(BF16).reshape(4, 64, TOK)
    if len(targets) > 1:
        targets[1][...] = rows.astype(BF16)


def turned(values, keep=False):
    shapes = [jax.ShapeDtypeStruct((4, 4, 2, 64, TOK), BF16)]
    specs = [pl.BlockSpec((1, 4, 1, 64, TOK), lambda z, x: (x, 0, z, 0, 0))]
    if keep:
        shapes.append(jax.ShapeDtypeStruct((TOK, D), BF16))
        specs.append(pl.BlockSpec((TOK, 256), lambda z, x: (0, z * 4 + x)))
    found = pl.pallas_call(
        turn_kernel,
        grid=(2, 4),
        in_specs=[pl.BlockSpec((TOK, 256), lambda z, x: (0, z * 4 + x))],
        out_specs=specs,
        out_shape=shapes,
        cost_estimate=pl.CostEstimate(flops=0, bytes_accessed=4 * TOK * D, transcendentals=0),
    )(values)
    rows = found[0].reshape(D, TOK)
    return (rows, found[1]) if keep else rows


def normalise(hidden):
    average = jnp.mean(hidden, axis=-1, keepdims=True)
    centred = hidden - average
    inv_std = lax.rsqrt(jnp.mean(centred * centred, axis=-1, keepdims=True) + EPSILON)
    return centred * inv_std, inv_std


def gelu_both(upward, grad_act):
    _, back = jax.vjp(partial(jax.nn.gelu, approximate=False), upward)
    return back(grad_act)[0].astype(BF16)


def attention(first_in, cot, qkv_weight, qkv_bias, dense_weight, segments, positions, order):
    heads = qkv_weight.shape[1] // (3 * HD)
    packed = (plain_dot(first_in, qkv_weight) + qkv_bias.reshape(-1)).reshape(TOK, heads, 3, HD)
    cosine, sine = angle_tables(positions)
    cosine = cosine[:, None, :]
    sine = sine[:, None, :]
    queries = rotate(packed[:, :, 0], cosine, sine).astype(BF16)
    keys_rot = rotate(packed[:, :, 1], cosine, sine).astype(BF16)
    values_in = packed[:, :, 2].astype(BF16)
    score_scale = 1.0 / math.sqrt(HD)
    scores = jnp.einsum("qhd,khd->hqk", queries, keys_rot, preferred_element_type=F32) * score_scale
    allowed = (segments[:, None] == segments[None, :]) & (order[None, :] <= order[:, None])
    scores = jnp.where(allowed[None], scores, NEGATIVE)
    top = jnp.max(scores, axis=-1, keepdims=True)
    weights = jnp.exp(scores - top)
    totals = jnp.sum(weights, axis=-1, keepdims=True)
    probs = weights / totals
    probs_low = probs.astype(BF16)
    mixed = jnp.einsum("hqk,khd->qhd", probs_low, values_in, preferred_element_type=F32)
    mixed_low = mixed.reshape(TOK, heads * HD).astype(BF16)

    grad_mixed = contract_cols(cot, dense_weight).astype(BF16).reshape(TOK, heads, HD)
    grad_probs = jnp.einsum("qhd,khd->hqk", grad_mixed, values_in, preferred_element_type=F32)
    along = jnp.sum(probs * grad_probs, axis=-1, keepdims=True)
    grad_scores = (probs * (grad_probs - along)).astype(BF16)
    grad_query = (
        jnp.einsum("hqk,khd->qhd", grad_scores, keys_rot, preferred_element_type=F32) * score_scale
    )
    grad_key = (
        jnp.einsum("hqk,qhd->khd", grad_scores, queries, preferred_element_type=F32) * score_scale
    )
    grad_value = jnp.einsum("hqk,qhd->khd", probs_low, grad_mixed, preferred_element_type=F32)
    grad_packed = jnp.stack(
        [rotate(grad_query, cosine, -sine), rotate(grad_key, cosine, -sine), grad_value], axis=2
    )
    return mixed_low, grad_packed.reshape(TOK, heads * 3 * HD).astype(BF16)


def body(
    hidden_in,
    segment_ids,
    positions,
    ln1_gain,
    ln1_bias,
    qkv_weight,
    qkv_bias,
    dense_weight,
    dense_bias,
    ln2_gain,
    ln2_bias,
    fc1_weight,
    fc1_bias,
    fc2_weight,
    fc2_bias,
    cotangent,
):
    core = lax.axis_index("c")
    side = lax.axis_index("zl")
    half_rows = TOK // 2
    half_units = fc1_weight.shape[1] // 2
    after = lax.optimization_barrier

    def of_core(values, which):
        return lax.dynamic_slice_in_dim(values, which * half_rows, half_rows, 0)

    def both_cores(mine):
        theirs = send(mine, "c")
        whole = jnp.zeros((TOK,) + mine.shape[1:], mine.dtype)
        whole = lax.dynamic_update_slice_in_dim(whole, mine, core * half_rows, 0)
        return lax.dynamic_update_slice_in_dim(whole, theirs, (1 - core) * half_rows, 0)

    def cut(values, width, axis):
        return lax.dynamic_slice_in_dim(values, side * width, width, axis)

    hidden_got = send(of_core(hidden_in, core).astype(F32), "zl")
    cot_got = send(of_core(cotangent, core).astype(F32), "zl")
    marks_got = send(jnp.stack([segment_ids, positions]), "zl")

    cot_rows = turned(cotangent)
    hidden = hidden_in.astype(F32)
    normed, inv_std = normalise(hidden)
    second_in = (normed * ln2_gain + ln2_bias).astype(BF16)
    upward = plain_dot(second_in, fc1_weight) + fc1_bias.reshape(-1)
    act_low = jax.nn.gelu(upward, approximate=False).astype(BF16)
    down_grad = plain_dot(cot_rows, act_low)
    down_sum = lax.psum_scatter(down_grad, ("x", "y"), scatter_dimension=0, tiled=True)
    _, cotangent, upward, hidden = after((down_grad, cotangent, upward, hidden))

    normed, inv_std = normalise(hidden)
    first_in = (normed * ln1_gain + ln1_bias).astype(BF16)
    second_rows = turned(second_in)
    first_rows = turned(first_in)
    grad_up = gelu_both(upward, contract_cols(cotangent, fc2_weight))
    mixed_low, grad_packed = attention(
        first_in,
        cotangent,
        qkv_weight,
        qkv_bias,
        dense_weight,
        segment_ids,
        positions,
        jnp.arange(TOK),
    )

    _, _, hidden_got, cot_got = after((grad_up, grad_packed, hidden_got, cot_got))
    hidden_far = jnp.concatenate([hidden_got, send(hidden_got, "c")], axis=0)
    cot_far = jnp.concatenate([cot_got, send(cot_got, "c")], axis=0)
    order_far = (jnp.arange(TOK) + core * half_rows) % TOK
    marks_far = jnp.concatenate(
        [lax.dynamic_slice_in_dim(marks_got, w * half_rows, half_rows, 1) for w in (core, 1 - core)],
        axis=1,
    )
    cot_far_rows, cot_far = turned(cot_far, keep=True)
    normed_far, _ = normalise(hidden_far)
    first_far = (normed_far * ln1_gain + ln1_bias).astype(BF16)
    second_far = (normed_far * ln2_gain + ln2_bias).astype(BF16)
    upward_far = plain_dot(second_far, cut(fc1_weight, half_units, 1)) + cut(
        fc1_bias.reshape(-1), half_units, 0
    )
    grad_up_far = gelu_both(upward_far, contract_cols(cot_far, cut(fc2_weight, half_units, 0)))
    mixed_far, grad_packed_far = attention(
        first_far,
        cot_far,
        cut(qkv_weight, 3 * HD, 1),
        cut(qkv_bias, 1, 0),
        cut(dense_weight, HD, 0),
        marks_far[0],
        marks_far[1],
        order_far,
    )
    second_far_rows = turned(second_far)
    first_far_rows = turned(first_far)

    def pair(own, far, width):
        return jnp.concatenate([cut(own, width, 1), far], axis=0)

    def beside(own, far):
        return jnp.concatenate([own, far], axis=1)

    widths = (half_units, HD, 3 * HD)
    joint_grad = jnp.concatenate(
        [
            plain_dot(beside(second_rows, second_far_rows), pair(grad_up, grad_up_far, widths[0])),
            plain_dot(beside(cot_rows, cot_far_rows), pair(mixed_low, mixed_far, widths[1])),
            plain_dot(beside(first_rows, first_far_rows), pair(grad_packed, grad_packed_far, widths[2])),
        ],
        axis=1,
    )
    joint_sum = lax.psum_scatter(joint_grad, ("x", "y"), scatter_dimension=0, tiled=True)
    _, mixed_low, act_low, grad_up, grad_packed = after(
        (joint_grad, mixed_low, act_low, grad_up, grad_packed)
    )

    def branch_half(which):
        return plain_dot(of_core(mixed_low, which), dense_weight) + plain_dot(
            of_core(act_low, which), fc2_weight
        )

    branch = branch_half(core) + send(branch_half(1 - core), "c")
    branch = branch + send(branch, "zh")
    output = both_cores(of_core(hidden, core) + branch + dense_bias + fc2_bias)

    first_part = contract_cols(grad_packed, qkv_weight)
    second_part = contract_cols(grad_up, fc1_weight)
    combined = first_part * ln1_gain + second_part * ln2_gain
    combined = of_core(combined, core) + send(of_core(combined, 1 - core), "c")
    combined = combined + send(combined, "zh")
    normed_half = of_core(normed, core)
    grad_out = cotangent.astype(F32)
    input_half = of_core(grad_out, core) + of_core(inv_std, core) * (
        combined
        - jnp.mean(combined, axis=-1, keepdims=True)
        - normed_half * jnp.mean(combined * normed_half, axis=-1, keepdims=True)
    )
    input_grad = both_cores(input_half)

    gain_one_grad = jnp.sum(first_part * normed, axis=0)
    shift_one_grad = jnp.sum(first_part, axis=0)
    gain_two_grad = jnp.sum(second_part * normed, axis=0)
    shift_two_grad = jnp.sum(second_part, axis=0)
    bias_sum = jnp.sum(grad_out, axis=0)
    qkv_bias_sum = jnp.sum(grad_packed.astype(F32), axis=0)
    up_bias_grad = jnp.sum(grad_up.astype(F32), axis=0)
    features = jnp.stack(
        [gain_one_grad, shift_one_grad, gain_two_grad, shift_two_grad, bias_sum]
    ).reshape(5, 32, 64)
    small = jnp.concatenate(
        [
            features.transpose(1, 0, 2).reshape(32, 320),
            qkv_bias_sum.reshape(2, 32, 24).transpose(1, 0, 2).reshape(32, 48),
            up_bias_grad.reshape(16, 32, 4).transpose(1, 0, 2).reshape(32, 64),
            jnp.zeros((32, 80), F32),
        ],
        axis=1,
    )
    small = lax.psum(small, ("x", "y"))
    block = lax.axis_index("x") * 4 + lax.axis_index("y")
    own_small = lax.dynamic_slice_in_dim(small, side * 16 + block, 1, 0)
    far_small = lax.dynamic_slice_in_dim(small, (1 - side) * 16 + block, 1, 0)
    small = (own_small + send(far_small, "zl")).reshape(-1)
    norms = small[:256]
    norms = norms + send(norms, "c")
    norms = (norms + send(norms, "zh")).reshape(4, 64)
    bias_total = small[256:320]

    def of_side(values, which):
        return lax.dynamic_slice_in_dim(values, which * 64, 64, 0)

    down_sum = of_side(down_sum, side) + send(of_side(down_sum, 1 - side), "zl")
    near = of_side(joint_sum, side)
    far = send(of_side(joint_sum, 1 - side), "zl")
    low = jnp.where(side == 0, near, far)
    high = jnp.where(side == 0, far, near)
    sums = []
    start = 0
    for width in widths:
        sums.append(
            jnp.concatenate([low[:, start : start + width], high[:, start : start + width]], axis=1)
        )
        start += width
    up_sum, dense_sum, qkv_sum = sums
    return (
        output,
        input_grad,
        norms[0],
        norms[1],
        qkv_sum,
        small[320:368].reshape(2, 24),
        dense_sum.T,
        bias_total,
        norms[2],
        norms[3],
        up_sum,
        small[368:432].reshape(16, 4),
        down_sum.T,
        bias_total,
    )


def solution(mesh):
    fine = Mesh(mesh.devices.reshape(tuple(SIZES.values())), tuple(SIZES))
    return jax.shard_map(
        body,
        mesh=fine,
        in_specs=(
            P(DP, None),
            P(DP),
            P(DP),
            P(),
            P(),
            P(None, TENSOR),
            P(TENSOR, None),
            P(TENSOR, None),
            P(),
            P(),
            P(),
            P(None, TENSOR),
            P(TENSOR, None),
            P(TENSOR, None),
            P(),
            P(DP, None),
        ),
        out_specs=(
            P(DP, None),
            P(DP, None),
            P(DP),
            P(DP),
            P(DP, TENSOR),
            P(TENSOR, DP),
            P(TENSOR, DP),
            P(DP),
            P(DP),
            P(DP),
            P(DP, TENSOR),
            P(TENSOR, DP),
            P(TENSOR, DP),
            P(DP),
        ),
        check_vma=False,
    )
```

time: 717 us -> 644 us (0.90)
  starting transfers between devices: 172 us -> 15.3 us
  local copies, waits for them, and re-layouts: 37.6 us -> 78.6 us
  other arithmetic: 42.9 us -> 79.7 us
  between operations: 2.9 us -> 15.3 us
  Pallas kernels: 29.4 us -> 37.8 us
    ppermute x125 -> x16, waiting for transfers between devices: 276 us -> 93.4 us  [send(): return lax.ppermute(value, axis, [(i, (i + step) % n) for i in range(n)])]
    reduce_scatter x0 -> x2, waiting for transfers between devices: none -> 175 us  [the longest x1 110 us: body(): lax.psum_scatter(joint_grad, ('x', 'y'), scatter_dimension=0, tiled=True)]
    ppermute x125 -> x16, starting transfers between devices: 172 us -> 15.2 us  [send(): return lax.ppermute(value, axis, [(i, (i + step) % n) for i in range(n)])]
    dot_general x70 -> x12, matrix products: 92.7 us -> 65.8 us  [plain_dot(): return jnp.dot(left, right, preferred_element_type=F32)]
    dot_general x4 -> x6, matrix products: 38.3 us -> 56.6 us  [contract_cols(): lax.dot_general(left, right, (((1,), (1,)), ((), ())), preferred_element_...]
    concatenate x5 -> x7, other arithmetic: 1.99 us -> 16.1 us  [the longest x1 7.31 us: body(): jnp.concatenate([plain_dot(beside(second_rows, second_far_rows), pair(gra...]
    dynamic_slice x0 -> x11, local copies, waits for them, and re-layouts: none -> 10.7 us  [the longest x4 5.34 us: of_side(): return lax.dynamic_slice_in_dim(values, which * 64, 64, 0)]
    reduce_sum x2 -> x8, other arithmetic: 2.77 us -> 12.2 us  [the longest x3 6.31 us: normalise(): jnp.mean(centred * centred, axis=-1, keepdims=True) + EPSILON]
  transfers between devices with their start and end apart: 125 -> 19, of which waited for: 48 -> 8; matrix products, arithmetic and copies ran while one was open for 24% -> 32% of each run, Pallas kernels for 3% -> 4%
where the time goes in v2:
time: 644 us; the launch traced here: 632 us
  waiting for transfers between devices  269 us (42%)
  matrix products  136 us (21%)
  other arithmetic  79.7 us (12%)
  local copies, waits for them, and re-layouts  78.6 us (12%)
  Pallas kernels  37.8 us (6%)
  starting transfers between devices  15.3 us (2%)
  between operations  15.3 us (2%)
    reduce_scatter x1, waiting for transfers between devices, body(): lax.psum_scatter(joint_grad, ('x', 'y'), scatter_dimension=0, tiled=True)  110 us
    ppermute x16, waiting for transfers between devices, send(): return lax.ppermute(value, axis, [(i, (i + step) % n) for i in range(n)])  93.4 us
    dot_general x12, matrix products, plain_dot(): return jnp.dot(left, right, preferred_element_type=F32)  65.8 us
    reduce_scatter x1, waiting for transfers between devices, body(): lax.psum_scatter(down_grad, ('x', 'y'), scatter_dimension=0, tiled=True)  65 us
    dot_general x6, matrix products, contract_cols(): lax.dot_general(left, right, (((1,), (1,)), ((), ())), preferred_element_...  56.6 us
    pallas_call x6, Pallas kernels, turned(): pl.pallas_call(turn_kernel, grid=(2, 4), in_specs=[pl.BlockSpec((TOK, 256...  37.8 us
    unnamed x158, local copies, waits for them, and re-layouts  24.3 us
    ppermute x16, starting transfers between devices, send(): return lax.ppermute(value, axis, [(i, (i + step) % n) for i in range(n)])  15.2 us
  transfers between devices with their start and end apart: 19, of which 8 were waited for; matrix products, arithmetic and copies ran while one was open for 32% of the time, Pallas kernels for 4%

profile of v2, /device:TPU:0, one launch (start us, length us, event | category | flops | bytes accessed | tf_op | source)
XLA Modules:
  0.0 632.5 jit_solution(13816032651030210915)
XLA Ops:
  19.1 6.2 shard_map.263
  25.3 4.3 convert_element_type.126
  32.8 17.5 %fusion.3 = (bf16[512,2048]{1,0:T(8,128)(2,1)S(1)}, f32[512,2048]{1,0:T(8,128)}) fusion(f32[2048]{0:T(1024)S(1)} %bitcast.164, bf16[512,2048]{1,0:T(8,128)(2,1)S(1)} %add_convert_fusion.3.source, bf16[2048,2048]{1,0:T(8,128)(2,1)} %param.27), kind=kOutput, calls=%fused_computation.7 | convolution fusion | flops 4364173312 | bytes 16785408 | tf_op jit(solution)/shard_map/dot_general | solution.py:45
  51.6 8.6 %convolution_bitcast_fusion = f32[2048,2048]{0,1:T(8,128)} fusion(bf16[512,2048]{1,0:T(8,128)(2,1)S(1)} %get-tuple-element.33, bf16[2048,512]{1,0:T(8,128)(2,1)S(1)} %bitcast.144), kind=kOutput, calls=%fused_computation.2 | convolution fusion | flops 4294967296 | bytes 20971520 | tf_op jit(solution)/shard_map/dot_general | solution.py:45
  70.5 7.9 %convolution_add_fusion = f32[512,1536]{1,0:T(8,128)} fusion(bf16[512,2048]{1,0:T(8,128)(2,1)S(1)} %get-tuple-element.89.source, bf16[2048,1536]{1,0:T(8,128)(2,1)} %param.21, f32[1536]{0:T(1024)S(1)} %add.280), kind=kOutput, calls=%fused_computation.72 | convolution fusion | flops 3222011904 | bytes 11540480 | tf_op jit(solution)/shard_map/dot_general | solution.py:45
  78.3 3.5 copy.84
  89.0 3.8 convolution_convert_fusion
  92.9 17.5 %fusion.8 = bf16[512,2048]{1,0:T(8,128)(2,1)} fusion(f32[512,2048]{1,0:T(8,128)S(1)} %copy-done.71, bf16[512,2048]{1,0:T(8,128)(2,1)S(1)} %copy-done.5, bf16[2048,2048]{1,0:T(8,128)(2,1)} %param.29), kind=kOutput, calls=%fused_computation.12 | convolution fusion | flops 4370464768 | bytes 16777216 | tf_op jit(solution)/shard_map/dot_general | solution.py:49
  127.3 4.0 fusion.164
  142.5 6.1 shard_map.264
  148.6 6.1 shard_map.267
  176.9 5.6 add_convert_fusion.1
  182.5 6.3 %shard_map.268 = bf16[4,4,2,64,512]{4,3,2,1,0:T(8,128)(2,1)} custom-call(bf16[512,2048]{1,0:T(8,128)(2,1)} %get-tuple-element.93.source), custom_call_target="tpu_custom_call" | custom-call | bytes 4194304 | tf_op jit(solution)/shard_map/pallas_call | solution.py:65
  188.8 5.5 fusion.63
  200.0 4.7 pad_maximum_fusion.1.source
  204.8 7.0 %shard_map.266 = (bf16[4,4,2,64,512]{4,3,2,1,0:T(8,128)(2,1)}, bf16[512,2048]{1,0:T(8,128)(2,1)}) custom-call(f32[512,2048]{1,0:T(8,128)} %pad_maximum_fusion.1.source), custom_call_target="tpu_custom_call" | custom-call | bytes 4194304 | tf_op jit(solution)/shard_map/pallas_call | solution.py:65
  220.4 3.7 fusion.23
  224.1 6.1 shard_map.265
  231.8 10.3 %fusion.46 = bf16[512,1024]{1,0:T(8,128)(2,1)S(1)} fusion(f32[512,1024]{1,0:T(8,128)} %fusion.23, bf16[512,2048]{1,0:T(8,128)(2,1)} %get-tuple-element.30, bf16[2048,2048]{1,0:T(8,128)(2,1)} %param.29, s32[]{:T(128)S(6)} %select_n.91, f32[1024]{0:T(1024)} %dynamic_slice.90), kind=kOutput, calls=%fused_computation.86 | convolution fusion | flops 2185756672 | bytes 9441284 | tf_op jit(solution)/shard_map/dot_general | solution.py:49
  244.6 3.4 fusion.17
  248.1 4.6 fusion.9
  252.7 7.3 %pad_maximum_fusion = f32[2048,2048]{0,1:T(8,128)} fusion(f32[2048,768]{0,1:T(8,128)S(1)} %fusion.17, f32[2048,256]{0,1:T(8,128)S(1)} %fusion.13, f32[2048,1024]{0,1:T(8,128)S(1)} %fusion.9), kind=kLoop, calls=%fused_computation.1 | loop fusion | flops 8388608 | bytes 33554432 | tf_op jit(solution)/shard_map/concatenate | solution.py:229
  261.7 8.9 %fusion.166 = f32[512,2048]{1,0:T(8,128)} fusion(bf16[512,1536]{0,1:T(8,128)(2,1)} %bitcast.133, bf16[2048,1536]{1,0:T(8,128)(2,1)} %param.21), kind=kOutput, calls=%fused_computation.322 | convolution fusion | flops 3221225472 | bytes 12058624 | tf_op jit(solution)/shard_map/dot_general | solution.py:49
  271.8 13.6 %fusion.160 = (f32[2048]{0:T(1024)S(1)}, f32[2048]{0:T(1024)S(1)}, f32[2048]{0:T(1024)S(1)}, f32[2048]{0:T(1024)S(1)}, f32[512,2048]{1,0:T(8,128)}) fusion(f32[512,2048]{1,0:T(8,128)} %get-tuple-element.90, f32[512,2048]{1,0:T(8,128)} %fusion.166, f32[2048]{0:T(1024)S(1)} %copy-done.49, f32[2048]{0:T(1024)S(1)} %copy-done.52, ...), kind=kOutput, calls=%fused_computation.316 | convolution fusion | flops 4304396288 | bytes 23117824 | tf_op jit(solution)/shard_map/dot_general | solution.py:49
  288.1 6.1 fusion.74
  297.1 5.7 fusion.76
  303.7 3.7 collective-permute-start.6
  308.3 45.4 %collective-permute-done.6 = f32[256,2048]{1,0:T(8,128)S(1)} collective-permute-done((f32[256,2048]{1,0:T(8,128)S(1)}, f32[256,2048]{1,0:T(8,128)S(1)}, u32[]{:S(2)}, u32[]{:S(2)}) %collective-permute-start.6) | collective-permute-done | bytes 2097184 | tf_op jit(solution)/shard_map/ppermute | solution.py:25
  356.4 41.7 %collective-permute-done.9 = f32[256,2048]{1,0:T(8,128)S(1)} collective-permute-done((f32[256,2048]{1,0:T(8,128)S(1)}, f32[256,2048]{1,0:T(8,128)S(1)}, u32[]{:S(2)}, u32[]{:S(2)}) %collective-permute-start.9) | collective-permute-done | bytes 2097184 | tf_op jit(solution)/shard_map/ppermute | solution.py:25
  403.9 3.6 collective-permute-done.11
  418.1 65.0 %reduce-scatter.5.cloned.1.call-done = f32[128,2048]{0,1:T(8,128)} async-done(((f32[2048,2048]{0,1:T(8,128)}), f32[128,2048]{0,1:T(8,128)}) %reduce-scatter.5.cloned.1.call-update) | async-done | bytes 1048592 | tf_op jit(solution)/shard_map/reduce_scatter | solution.py:174
  487.4 109.6 %reduce-scatter.3.cloned.1.call-done = f32[128,2048]{0,1:T(8,128)} async-done(((f32[2048,2048]{0,1:T(8,128)}), f32[128,2048]{0,1:T(8,128)}) %reduce-scatter.3.cloned.1.call-update) | async-done | bytes 1048592 | tf_op jit(solution)/shard_map/reduce_scatter | solution.py:237
  (336 shorter events, 163.8 us)
Async XLA Ops:
  7.2 81.8 %copy-start = (bf16[512,2048]{1,0:T(8,128)(2,1)S(1)}, bf16[512,2048]{1,0:T(8,128)(2,1)}, u32[]{:S(2)}) copy-start(bf16[512,2048]{1,0:T(8,128)(2,1)} %param.23) | copy-start | bytes 6291460
  7.2 395.9 %all-reduce.2.cloned.1.call-start = ((), (), s32[]{:S(2)}) async-start(), calls=%async_computation.2 | async-start | bytes 131072 | tf_op jit(solution)/shard_map/psum | solution.py:284
  8.1 111.4 %collective-permute-start.4 = (s32[2,512]{1,0:T(2,128)S(1)}, s32[2,512]{1,0:T(2,128)S(1)}, u32[]{:S(2)}, u32[]{:S(2)}) collective-permute-start(s32[2,512]{1,0:T(2,128)S(1)} %pad_add_fusion), channel_id=1, source_target_pairs={{0,64},{64,0},{1,65},{65,1},{2,66},{66,2},{3,67},{67,3},{4,68},{68... | collective-permute-start | bytes 12296 | tf_op jit(solution)/shard_map/ppermute | solution.py:25
  13.0 129.3 %collective-permute-start = (f32[256,2048]{1,0:T(8,128)}, f32[256,2048]{1,0:T(8,128)}, u32[]{:S(2)}, u32[]{:S(2)}) collective-permute-start(f32[256,2048]{1,0:T(8,128)} %dynamic-slice_convert_fusion.1), channel_id=1, source_target_pairs={{0,64},{64,0},{1,65},{65,1},{2,66},{66,2},{3,67},{67,3},{4,68},{68... | collective-permute-start | bytes 6291464 | tf_op jit(solution)/shard_map/ppermute | solution.py:25
  15.8 126.5 %collective-permute-start.1 = (f32[256,2048]{1,0:T(8,128)}, f32[256,2048]{1,0:T(8,128)}, u32[]{:S(2)}, u32[]{:S(2)}) collective-permute-start(f32[256,2048]{1,0:T(8,128)} %dynamic-slice_convert_fusion), channel_id=1, source_target_pairs={{0,64},{64,0},{1,65},{65,1},{2,66},{66,2},{3,67},{67,3},{4,68},{68... | collective-permute-start | bytes 6291464 | tf_op jit(solution)/shard_map/ppermute | solution.py:25
  32.7 17.5 %copy-start.11 = (bf16[512,2048]{1,0:T(8,128)(2,1)}, bf16[512,2048]{1,0:T(8,128)(2,1)S(1)}, u32[]{:S(2)}) copy-start(bf16[512,2048]{1,0:T(8,128)(2,1)S(1)} %add_convert_fusion.3.source) | copy-start | bytes 6291460
  32.8 18.9 %copy-start.20 = (bf16[4,4,2,64,512]{4,3,2,1,0:T(8,128)(2,1)S(1)}, bf16[4,4,2,64,512]{4,3,2,1,0:T(8,128)(2,1)}, u32[]{:S(2)}) copy-start(bf16[4,4,2,64,512]{4,3,2,1,0:T(8,128)(2,1)} %shard_map.263) | copy-start | bytes 6291460
  92.8 17.6 %copy-start.9 = (f32[512,2,1,256]{3,0,1,2:T(8,128)S(1)}, f32[512,2,1,256]{3,0,1,2:T(8,128)}, u32[]{:S(2)}) copy-start(f32[512,2,1,256]{3,0,1,2:T(8,128)} %copy.131) | copy-start | bytes 3145732
  142.4 26.1 %collective-permute-start.2 = (f32[256,2048]{1,0:T(8,128)}, f32[256,2048]{1,0:T(8,128)}, u32[]{:S(2)}, u32[]{:S(2)}) collective-permute-start(f32[256,2048]{1,0:T(8,128)} %collective-permute-done), channel_id=1, source_target_pairs={{0,1},{1,0},{2,3},{3,2},{4,5},{5,4},{6,7},{7,6},{8,9},{9,8},{10,11... | collective-permute-start | bytes 6291464 | tf_op jit(solution)/shard_map/ppermute | solution.py:25
  164.8 35.2 %collective-permute-start.3 = (f32[256,2048]{1,0:T(8,128)}, f32[256,2048]{1,0:T(8,128)}, u32[]{:S(2)}, u32[]{:S(2)}) collective-permute-start(f32[256,2048]{1,0:T(8,128)} %collective-permute-done.1), channel_id=1, source_target_pairs={{0,1},{1,0},{2,3},{3,2},{4,5},{5,4},{6,7},{7,6},{8,9},{9,8},{10,11... | collective-permute-start | bytes 6291464 | tf_op jit(solution)/shard_map/ppermute | solution.py:25
  231.8 10.3 %copy-start.21 = (bf16[4,4,2,64,512]{4,3,2,1,0:T(8,128)(2,1)S(1)}, bf16[4,4,2,64,512]{4,3,2,1,0:T(8,128)(2,1)}, u32[]{:S(2)}) copy-start(bf16[4,4,2,64,512]{4,3,2,1,0:T(8,128)(2,1)} %shard_map.263) | copy-start | bytes 6291460
  271.7 14.1 %copy-start.58 = (f32[512]{0:T(512)S(1)}, f32[512]{0:T(512)}, u32[]{:S(2)}) copy-start(f32[512]{0:T(512)} %pad.9.clone) | copy-start | bytes 6148
  286.6 196.6 %reduce-scatter.5.cloned.1.call-start = ((), (), s32[]{:S(2)}) async-start(), calls=%async_computation.4 | async-start | bytes 17825792 | tf_op jit(solution)/shard_map/reduce_scatter | solution.py:174
  287.4 309.7 %reduce-scatter.3.cloned.1.call-start = ((), (), s32[]{:S(2)}) async-start(), calls=%async_computation.3 | async-start | bytes 17825792 | tf_op jit(solution)/shard_map/reduce_scatter | solution.py:237
  295.0 7.9 %collective-permute-start.5 = (f32[256,2048]{1,0:T(8,128)S(1)}, f32[256,2048]{1,0:T(8,128)S(1)}, u32[]{:S(2)}, u32[]{:S(2)}) collective-permute-start(f32[256,2048]{1,0:T(8,128)S(1)} %convolution_add_fusion.2), channel_id=1, source_target_pairs={{0,1},{1,0},{2,3},{3,2},{4,5},{5,4},{6,7},{7,6},{8,9},{9,8},{10,11... | collective-permute-start | bytes 6291464 | tf_op jit(solution)/shard_map/ppermute | solution.py:25
  296.6 10.7 %collective-permute-start.8 = (f32[256,2048]{1,0:T(8,128)S(1)}, f32[256,2048]{1,0:T(8,128)S(1)}, u32[]{:S(2)}, u32[]{:S(2)}) collective-permute-start(f32[256,2048]{1,0:T(8,128)S(1)} %constant_dynamic-slice_fusion.4), channel_id=1, source_target_pairs={{0,1},{1,0},{2,3},{3,2},{4,5},{5,4},{6,7},{7,6},{8,9},{9,8},{10,11... | collective-permute-start | bytes 6291464 | tf_op jit(solution)/shard_map/ppermute | solution.py:25
  303.7 50.1 %collective-permute-start.6 = (f32[256,2048]{1,0:T(8,128)S(1)}, f32[256,2048]{1,0:T(8,128)S(1)}, u32[]{:S(2)}, u32[]{:S(2)}) collective-permute-start(f32[256,2048]{1,0:T(8,128)S(1)} %fusion.41), channel_id=1, source_target_pairs={{0,2},{2,0},{1,3},{3,1},{4,6},{6,4},{5,7},{7,5},{8,10},{10,8},{9,1... | collective-permute-start | bytes 6291464 | tf_op jit(solution)/shard_map/ppermute | solution.py:25
  307.6 90.6 %collective-permute-start.9 = (f32[256,2048]{1,0:T(8,128)S(1)}, f32[256,2048]{1,0:T(8,128)S(1)}, u32[]{:S(2)}, u32[]{:S(2)}) collective-permute-start(f32[256,2048]{1,0:T(8,128)S(1)} %dynamic-slice_add_fusion), channel_id=1, source_target_pairs={{0,2},{2,0},{1,3},{3,1},{4,6},{6,4},{5,7},{7,5},{8,10},{10,8},{9,1... | collective-permute-start | bytes 6291464 | tf_op jit(solution)/shard_map/ppermute | solution.py:25
  307.8 46.5 %copy-start.2 = (f32[512,2048]{1,0:T(8,128)S(1)}, f32[512,2048]{1,0:T(8,128)}, u32[]{:S(2)}) copy-start(f32[512,2048]{1,0:T(8,128)} %convert_element_type.126) | copy-start | bytes 12582916
  307.8 46.5 %copy-start.60 = (f32[2048]{0:T(1024)S(1)}, f32[2048]{0:T(1024)}, u32[]{:S(2)}) copy-start(f32[2048]{0:T(1024)} %param.30) | copy-start | bytes 24580
  307.8 46.5 %copy-start.61 = (f32[2048]{0:T(1024)S(1)}, f32[2048]{0:T(1024)}, u32[]{:S(2)}) copy-start(f32[2048]{0:T(1024)} %param.24) | copy-start | bytes 24580
  354.3 43.9 %copy-start.7 = (f32[512,2048]{1,0:T(8,128)S(1)}, f32[512,2048]{1,0:T(8,128)}, u32[]{:S(2)}) copy-start(f32[512,2048]{1,0:T(8,128)} %get-tuple-element.90) | copy-start | bytes 12582916
  356.4 42.2 %copy-start.18 = (f32[512,2048]{1,0:T(8,128)}, f32[512,2048]{1,0:T(8,128)S(1)}, u32[]{:S(2)}) copy-start(f32[512,2048]{1,0:T(8,128)S(1)} %get-tuple-element.87) | copy-start | bytes 12582916
  356.4 58.6 %collective-permute-start.7 = (f32[256,2048]{1,0:T(8,128)}, f32[256,2048]{1,0:T(8,128)}, u32[]{:S(2)}, u32[]{:S(2)}) collective-permute-start(f32[256,2048]{1,0:T(8,128)} %get-tuple-element.88), channel_id=1, source_target_pairs={{0,1},{1,0},{2,3},{3,2},{4,5},{5,4},{6,7},{7,6},{8,9},{9,8},{10,11... | collective-permute-start | bytes 6291464 | tf_op jit(solution)/shard_map/ppermute | solution.py:25
  403.1 198.2 %collective-permute-start.10 = (f32[256,2048]{1,0:T(8,128)}, f32[256,2048]{1,0:T(8,128)}, u32[]{:S(2)}, u32[]{:S(2)}) collective-permute-start(f32[256,2048]{1,0:T(8,128)} %get-tuple-element.85), channel_id=1, source_target_pairs={{0,1},{1,0},{2,3},{3,2},{4,5},{5,4},{6,7},{7,6},{8,9},{9,8},{10,11... | collective-permute-start | bytes 6291464 | tf_op jit(solution)/shard_map/ppermute | solution.py:25
  403.9 3.6 collective-permute-start.11
  408.2 1.1 collective-permute-start.12
  408.3 216.8 %copy-start.65 = (f32[64]{0:T(128)}, f32[64]{0:T(128)S(1)}, u32[]{:S(2)}) copy-start(f32[64]{0:T(128)S(1)} %get-tuple-element.178) | copy-start | bytes 772
  409.3 5.1 collective-permute-start.13
  485.9 118.6 %collective-permute-start.15 = (f32[64,2048]{1,0:T(8,128)}, f32[64,2048]{1,0:T(8,128)}, u32[]{:S(2)}, u32[]{:S(2)}) collective-permute-start(f32[64,2048]{1,0:T(8,128)} %copy.112), channel_id=1, source_target_pairs={{0,64},{64,0},{1,65},{65,1},{2,66},{66,2},{3,67},{67,3},{4,68},{68... | collective-permute-start | bytes 1572872 | tf_op jit(solution)/shard_map/ppermute | solution.py:25
  599.7 13.7 %collective-permute-start.14 = (f32[64,2048]{1,0:T(8,128)}, f32[64,2048]{1,0:T(8,128)}, u32[]{:S(2)}, u32[]{:S(2)}) collective-permute-start(f32[64,2048]{1,0:T(8,128)} %copy.109), channel_id=1, source_target_pairs={{0,64},{64,0},{1,65},{65,1},{2,66},{66,2},{3,67},{67,3},{4,68},{68... | collective-permute-start | bytes 1572872 | tf_op jit(solution)/shard_map/ppermute | solution.py:25
  604.5 11.3 %copy-start.15 = (f32[128,2048]{0,1:T(8,128)S(1)}, f32[128,2048]{0,1:T(8,128)}, u32[]{:S(2)}) copy-start(f32[128,2048]{0,1:T(8,128)} %reduce-scatter.3.cloned.1.call-done) | copy-start | bytes 3145732
  (61 other events, 249.6 us)
Sparse Core Ops, SparseCore 0:
  286.7 82.6 all-reduce.1
  373.2 109.9 reduce-scatter.4
  487.0 110.0 reduce-scatter.2
